TPU v7x, 32 devices: a whole 2x2x4 slice. The times are simulated.
32 devices in a mesh: grp: 4 (over z), feat: 8 (over y, x, core).
Axes of the slice: x: 2, y: 2, z: 4, core: 2. Of those that a mesh axis runs over, the one named last changes fastest.
Arguments:
- features: bfloat16 [4, 192, 768, 128], P('grp', None, 'feat'), may hold values from -6 to 6
- adj_tiles: bfloat16 [4, 96, 128, 128], P('grp'), may hold values from -0.4375 to 0.4375
- tile_rows: int32 [4, 96], P('grp'), may hold values from 0 to 63, as said below
- tile_cols: int32 [4, 96], P('grp'), may hold values from 0 to 191
- self_blocks: int32 [4, 64], P('grp'), may hold values from 0 to 191, as said below
- weight: bfloat16 [1536, 1024], replicated, may hold values from -0.15625 to 0.15625
- proj_bias: float32 [1024], replicated, may hold values from -0.5 to 0.5
- cotangent: bfloat16 [4, 8192, 1024], P('grp', 'feat'), may hold values from -0.03125 to 0.03125
Outputs:
- hidden: bfloat16 [4, 8192, 1024], P('grp', 'feat')
- weight_grad: float32 [1536, 1024], P('feat')
Inputs may be any that keep to these rules, and one draw needn't show every extreme that they name: `tile_rows`: within each minibatch the row blocks are in nondecreasing order and every row block 0 to 63 has at least one tile. `self_blocks`: within each minibatch the blocks are distinct.
All inputs are finite; a program needn't handle non-finite values.
Results may differ from a plain program's by a relative error of at most 0.0038.
Values may be sent and summed in bfloat16 or wider, within the bound.
A program may use at most 128 MiB of HBM per device.

v0:
```python
import jax
import jax.numpy as jnp
from jax import lax
from jax.sharding import PartitionSpec as P


def elu_act(value):
    return jnp.where(value > 0, value, jnp.expm1(jnp.minimum(value, 0.0)))


def per_device(
    features, adj_tiles, tile_rows, tile_cols, self_blocks, weight, proj_bias, cotangent
):
    local_blocks = features[0]
    col_count = local_blocks.shape[1]
    tile_side = local_blocks.shape[2]
    tile_count = adj_tiles.shape[1]
    block_count = self_blocks.shape[1]
    picked = jnp.take(local_blocks, tile_cols[0], axis=0)
    contrib = jnp.einsum("tfs,tds->tfd", picked, adj_tiles[0], preferred_element_type=jnp.float32)
    onehot = (tile_rows[0][None, :] == jnp.arange(block_count, dtype=jnp.int32)[:, None]).astype(
        jnp.float32
    )
    summed = jnp.dot(
        onehot, contrib.reshape(tile_count, col_count * tile_side), precision=lax.Precision.HIGHEST
    )
    aggregate = summed.reshape(block_count, col_count, tile_side).astype(jnp.bfloat16)
    self_feat = jnp.take(local_blocks, self_blocks[0], axis=0)
    stacked = jnp.stack([self_feat, aggregate], axis=1)
    owned = lax.all_to_all(stacked, "feat", split_axis=0, concat_axis=2, tiled=True)
    own_blocks = owned.shape[0]
    combined = owned.reshape(own_blocks, 2 * owned.shape[2], tile_side)
    preact = jnp.einsum("rcd,ch->rdh", combined, weight, preferred_element_type=jnp.float32)
    preact = preact.reshape(own_blocks * tile_side, weight.shape[1]) + proj_bias
    hidden = elu_act(preact).astype(jnp.bfloat16)
    pre_grad = (cotangent[0].astype(jnp.float32) * jnp.exp(jnp.minimum(preact, 0.0))).astype(
        jnp.bfloat16
    )
    grad_rows3 = pre_grad.reshape(own_blocks, tile_side, weight.shape[1])
    row_share = combined.shape[1] // lax.axis_size("feat")
    partial_grad = jnp.einsum(
        "rcd,rdh->ch", combined, grad_rows3, preferred_element_type=jnp.float32
    )
    totals = lax.psum(partial_grad, ("grp", "feat"))
    weight_grad = lax.dynamic_slice_in_dim(totals, lax.axis_index("feat") * row_share, row_share, 0)
    return (hidden[None], weight_grad)


def solution(mesh):
    return jax.shard_map(
        per_device,
        mesh=mesh,
        in_specs=(
            P("grp", None, "feat", None),
            P("grp", None, None, None),
            P("grp", None),
            P("grp", None),
            P("grp", None),
            P(),
            P(),
            P("grp", "feat", None),
        ),
        out_specs=(P("grp", "feat", None), P("feat", None)),
        check_vma=False,
    )
```

profile of v0, /device:TPU:0, one launch (start us, length us, event | category | flops | bytes accessed | tf_op | source)
XLA Modules:
  0.0 259.5 jit_solution(13322370965156174994)
XLA Ops:
  7.2 0.0 copy-start
  7.2 0.0 all-reduce.2.cloned.1.call-start
  7.2 0.8 fusion.21
  8.0 0.8 compare_and_fusion
  8.8 0.7 fusion.20
  9.5 0.7 compare_and_fusion.1
  10.1 4.7 %gather_fusion.1 = bf16[96,96,128]{2,1,0:T(8,128)(2,1)} fusion(bf16[192,96,128]{2,1,0:T(8,128)(2,1)} %bitcast.64, s32[1024]{0:T(1024)S(1)} %pad_clamp_fusion), kind=kCustom, calls=%fused_computation.1 | custom fusion | bytes 4718976 | tf_op jit(solution)/shard_map/jit(_take)/gather | solution.py:19
  14.8 4.2 %gather_fusion = bf16[64,96,128]{2,1,0:T(8,128)(2,1)} fusion(bf16[192,96,128]{2,1,0:T(8,128)(2,1)} %bitcast.65, s32[1024]{0:T(1024)S(1)} %pad_clamp_fusion.1), kind=kCustom, calls=%fused_computation | custom fusion | bytes 3145984 | tf_op jit(solution)/shard_map/jit(_take)/gather | solution.py:28
  19.0 0.0 copy-start.3
  19.0 4.9 %fusion.5 = f32[96,96,128]{2,1,0:T(8,128)S(1)} fusion(bf16[1,96,128,128]{3,2,1,0:T(8,128)(2,1)} %param.9, bf16[96,96,128]{2,1,0:T(8,128)(2,1)} %gather_fusion.1, pred[96]{0:T(512)(128)(4,1)S(1)} %compare_and_fusion), kind=kOutput, calls=%fused_computation.12 | convolution fusion | flops 303169536 | bytes 10223712 | tf_op jit(solution)/shard_map/tfs,tds->tfd/dot_general | solution.py:20
  24.0 0.0 copy-done.3
  24.0 0.0 copy-start.2
  24.0 4.9 %fusion.13 = bf16[64,1,96,128]{3,0,2,1:T(8,128)(2,1)S(1)} fusion(s32[96]{0:T(128)S(1)} %bitcast.67, f32[12,8,96,128]{3,2,1,0:T(8,128)S(1)} %bitcast.60), kind=kOutput, calls=%fused_computation.19 | convolution fusion | flops 906762240 | bytes 6291840 | tf_op jit(solution)/shard_map/dot_general | solution.py:24
  29.0 0.0 copy-done.2
  29.0 0.6 bitcast_select_fusion
  29.5 0.3 pad_maximum_fusion
  29.8 2.0 copy.17
  31.9 42.8 %all_to_all.15 = bf16[64,2,96,128]{3,2,1,0:T(8,128)(2,1)S(1)} all-to-all(bf16[64,2,96,128]{3,2,1,0:T(8,128)(2,1)S(1)} %copy.17), channel_id=1, replica_groups=mesh['grp'=4,'feat'=8] {'feat'}, dimensions={0} | all-to-all | bytes 6291456 | tf_op jit(solution)/shard_map/all_to_all | solution.py:30
  74.7 2.0 copy.18
  76.7 0.0 copy-start.4
  76.7 4.7 %copy.19 = bf16[8,128,1536]{2,1,0:T(8,128)(2,1)} copy(bf16[8,128,1536]{1,2,0:T(8,128)(2,1)} %bitcast.61) | data formatting | bytes 6291456 | tf_op jit(solution)/shard_map/rcd,ch->rdh/dot_general | solution.py:33
  81.3 0.0 copy-done
  81.3 0.0 copy-done.4
  81.3 0.0 copy-start.1
  81.3 8.5 %fusion.4 = (bf16[1024,1024]{1,0:T(8,128)(2,1)S(1)}, bf16[1,1024,1024]{2,1,0:T(8,128)(2,1)}) fusion(bf16[1,1024,1024]{2,1,0:T(8,128)(2,1)} %param.15, f32[1024]{0:T(1024)S(1)} %copy-done.4, bf16[1024,1536]{1,0:T(8,128)(2,1)} %bitcast.66, bf16[1536,1024]{1,0:T(8,128)(2,1)S(1)} %copy-done), kind=kOutput, calls=%fused_computation.10 | convolution fusion | flops 3229614080 | bytes 12587008 | tf_op jit(solution)/shard_map/rcd,ch->rdh/dot_general | solution.py:33
  89.9 0.0 copy-done.1
  89.9 5.2 %convolution_bitcast_fusion = f32[1536,1024]{1,0:T(8,128)} fusion(bf16[8,1536,128]{2,1,0:T(8,128)(2,1)S(1)} %bitcast.62, bf16[8,128,1024]{2,1,0:T(8,128)(2,1)S(1)} %bitcast.68), kind=kOutput, calls=%fused_computation.7 | convolution fusion | flops 3221225472 | bytes 11534336 | tf_op jit(solution)/shard_map/rcd,rdh->ch/dot_general | solution.py:41
  95.1 0.0 all-reduce.2.cloned.1.call-update
  95.1 155.4 %all-reduce.2.cloned.1.call-done = f32[1536,1024]{1,0:T(8,128)} async-done(((f32[1536,1024]{1,0:T(8,128)}), f32[1536,1024]{1,0:T(8,128)}) %all-reduce.2.cloned.1.call-update) | async-done | bytes 6291472 | tf_op jit(solution)/shard_map/psum | solution.py:44
  250.6 2.1 constant_dynamic-slice_fusion
  (2 shorter events, 0.0 us)
Async XLA Ops:
  7.2 74.2 %copy-start = (bf16[1536,1024]{1,0:T(8,128)(2,1)S(1)}, bf16[1536,1024]{1,0:T(8,128)(2,1)}, u32[]{:S(2)}) copy-start(bf16[1536,1024]{1,0:T(8,128)(2,1)} %param.13) | copy-start | bytes 9437188
  7.2 243.4 %all-reduce.2.cloned.1.call-start = ((), (), s32[]{:S(2)}) async-start(), calls=%async_computation.1 | async-start | bytes 12582912 | tf_op jit(solution)/shard_map/psum | solution.py:44
  19.0 5.0 %copy-start.3 = (s32[1,96]{1,0:T(1,128)S(1)}, s32[1,96]{1,0:T(1,128)}, u32[]{:S(2)}) copy-start(s32[1,96]{1,0:T(1,128)} %param.10) | copy-start | bytes 1156
  24.0 5.0 %copy-start.2 = (bf16[64,96,128]{2,1,0:T(8,128)(2,1)S(1)}, bf16[64,96,128]{2,1,0:T(8,128)(2,1)}, u32[]{:S(2)}) copy-start(bf16[64,96,128]{2,1,0:T(8,128)(2,1)} %gather_fusion) | copy-start | bytes 4718596
  76.7 4.7 %copy-start.4 = (f32[1024]{0:T(1024)S(1)}, f32[1024]{0:T(1024)}, u32[]{:S(2)}) copy-start(f32[1024]{0:T(1024)} %param.14) | copy-start | bytes 12292
  81.3 8.5 %copy-start.1 = (bf16[8,8,2,96,128]{4,3,0,2,1:T(8,128)(2,1)S(1)}, bf16[8,8,2,96,128]{4,3,0,2,1:T(8,128)(2,1)}, u32[]{:S(2)}) copy-start(bf16[8,8,2,96,128]{4,3,0,2,1:T(8,128)(2,1)} %copy.18) | copy-start | bytes 9437188
Sparse Core Ops, SparseCore 0:
  95.2 155.2 all-reduce.1
where the time goes:
time: 260 us
  waiting for transfers between devices  155 us (60%)
  blocking collectives  42.8 us (16%)
  matrix products  23.6 us (9%)
  local copies, waits for them, and re-layouts  19.7 us (8%)
  between operations  14.1 us (5%)
  other arithmetic  3.76 us (1%)
    psum x1, waiting for transfers between devices, per_device(): totals = lax.psum(partial_grad, ('grp', 'feat'))  155 us
    all_to_all x1, blocking collectives, per_device(): lax.all_to_all(stacked, 'feat', split_axis=0, concat_axis=2, tiled=True)  42.8 us
    dot_general x1, matrix products, per_device(): jnp.einsum('rcd,ch->rdh', combined, weight, preferred_element_type=jnp.fl...  8.52 us
    dot_general x1, matrix products, per_device(): jnp.einsum('rcd,rdh->ch', combined, grad_rows3, preferred_element_type=jn...  5.24 us
  transfers between devices with their start and end apart: 1, of which 1 were waited for; matrix products, arithmetic and copies ran while one was open for 0% of the time, Pallas kernels for 0%

commit v1 on v0

v1 whole, which is shorter than its diff:
```python
import functools

import jax
import jax.numpy as jnp
from jax import lax
from jax.experimental import pallas as pl
from jax.experimental.pallas import tpu as pltpu
from jax.sharding import PartitionSpec as P

MESH = pl.DeviceIdType.MESH
PIECES = 3
VMEM_BYTES = 56 * 1024 * 1024


def exchange_kernel(
    n, cols_ref, keep_ref, last_ref, blocks_ref, feat_ref, adj_ref, comb_ref,
    sendbuf, recvbuf, scan, send_sem, recv_sem,
):
    me = lax.axis_index("feat")
    rows = sendbuf.shape[2]
    width = feat_ref.shape[1]
    tiles = adj_ref.shape[0]

    barrier = pltpu.get_barrier_semaphore()

    def greet(i, carry):
        pl.semaphore_signal(
            barrier, inc=1, device_id={"feat": lax.rem(me + i, n)}, device_id_type=MESH
        )
        return carry

    lax.fori_loop(1, n, greet, 0)

    def fill_self(i, carry):
        peer = lax.rem(me + i, n)
        for r in range(rows):
            sendbuf[i, 0, r] = feat_ref[blocks_ref[peer * rows + r]]
        return carry

    def copy_to(i, kind):
        return pltpu.make_async_remote_copy(
            src_ref=sendbuf.at[i, kind],
            dst_ref=recvbuf.at[me, kind],
            send_sem=send_sem.at[i, kind],
            recv_sem=recv_sem.at[me, kind],
            device_id={"feat": lax.rem(me + i, n)},
            device_id_type=MESH,
        )

    def send_self(i, carry):
        fill_self(i, carry)
        copy_to(i, 0).start()
        return carry

    fill_self(1, 0)
    pl.semaphore_wait(barrier, n - 1)
    copy_to(1, 0).start()
    lax.fori_loop(2, n, send_self, 0)
    for r in range(rows):
        recvbuf[me, 0, r] = feat_ref[blocks_ref[me * rows + r]]

    def tile_terms(step, carry):
        for k in range(8):
            t = step * 8 + k
            scan[t] = lax.dot_general(
                feat_ref[cols_ref[t]], adj_ref[t], (((1,), (1,)), ((), ())),
                preferred_element_type=jnp.float32,
            )
        return carry

    lax.fori_loop(0, tiles // 8, tile_terms, 0)

    def running_sums(step, acc):
        for k in range(8):
            t = step * 8 + k
            acc = scan[t] + keep_ref[t] * acc
            scan[t] = acc
        return acc

    lax.fori_loop(0, tiles // 8, running_sums, jnp.zeros((width, 128), jnp.float32))

    def send_agg(i, carry):
        peer = lax.rem(me + i, n)
        for r in range(rows):
            sendbuf[i, 1, r] = scan[last_ref[peer * rows + r]].astype(jnp.bfloat16)
        copy_to(i, 1).start()
        return carry

    lax.fori_loop(1, n, send_agg, 0)
    for r in range(rows):
        recvbuf[me, 1, r] = scan[last_ref[me * rows + r]].astype(jnp.bfloat16)

    def wait_in(i, carry):
        src = lax.rem(me - i + n, n)
        for kind in range(2):
            pltpu.make_async_remote_copy(
                src_ref=sendbuf.at[i, kind],
                dst_ref=recvbuf.at[src, kind],
                send_sem=send_sem.at[i, kind],
                recv_sem=recv_sem.at[src, kind],
                device_id={"feat": lax.rem(me + i, n)},
                device_id_type=MESH,
            ).wait_recv()
        return carry

    lax.fori_loop(1, n, wait_in, 0)

    for kind in range(2):
        base = kind * n * width
        for r in range(rows):
            lanes = pl.ds(r * 128, 128)
            if width % 16 == 0:
                for src in range(n):
                    comb_ref[pl.ds(base + src * width, width), lanes] = recvbuf[src, kind, r]
            else:
                whole = jnp.concatenate(
                    [recvbuf[src, kind, r].astype(jnp.float32) for src in range(n)], axis=0
                )
                comb_ref[pl.ds(base, n * width), lanes] = whole.astype(jnp.bfloat16)

    def wait_out(i, carry):
        for kind in range(2):
            copy_to(i, kind).wait_send()
        return carry

    lax.fori_loop(1, n, wait_out, 0)


def layer_kernel(
    n, nz, comb_ref, w_ref, bias_ref, cot_ref, hid_ref, grad_ref,
    pg, lhs, picked, mine, pair_out, pair_in, own, chip_out, chip_in, red, z_out, z_in, g_out, g_in,
    pair_sem, chip_ssem, chip_rsem, z_ssem, z_rsem, g_ssem, g_rsem,
):
    me = lax.axis_index("feat")
    mz = lax.axis_index("grp")
    nc = n // 2
    chip, core = me // 2, lax.rem(me, 2)
    sibling = chip * 2 + (1 - core)
    share = grad_ref.shape[0]
    piece = share // PIECES
    hid = grad_ref.shape[1]
    cw = hid // nz

    def chip_at(i):
        return lax.rem(chip + i, nc) * 2 + core

    def z_at(i):
        return lax.rem(mz + i, nz)

    barrier = pltpu.get_barrier_semaphore()
    pl.semaphore_signal(barrier, inc=1, device_id={"feat": sibling}, device_id_type=MESH)
    for i in range(1, nc):
        pl.semaphore_signal(barrier, inc=1, device_id={"feat": chip_at(i)}, device_id_type=MESH)
    for i in range(1, nz):
        pl.semaphore_signal(barrier, inc=1, device_id={"grp": z_at(i)}, device_id_type=MESH)

    nodes = comb_ref.shape[1]
    step_nodes = 256
    step_cols = 256

    def forward(step, carry):
        at = pl.ds(pl.multiple_of(step * step_nodes, step_nodes), step_nodes)
        lhs[...] = comb_ref[:, at].T

        def forward_columns(k, inner):
            some = pl.ds(pl.multiple_of(k * step_cols, step_cols), step_cols)
            pre = jnp.dot(lhs[...], w_ref[:, some], preferred_element_type=jnp.float32)
            pre = pre + bias_ref[:, some]
            decay = jnp.exp(jnp.minimum(pre, 0.0))
            hid_ref[at, some] = jnp.where(pre > 0, pre, decay - 1.0).astype(jnp.bfloat16)
            pg[at, some] = (cot_ref[at, some].astype(jnp.float32) * decay).astype(jnp.bfloat16)
            return inner

        return lax.fori_loop(0, hid // step_cols, forward_columns, carry)

    lax.fori_loop(0, nodes // step_nodes, forward, 0)
    pl.semaphore_wait(barrier, 1 + (nc - 1) + (nz - 1))

    def terms(p, parity, out):
        for i in range(nc):
            owner = lax.rem(chip + i, nc) * 2 + parity
            at = pl.multiple_of(owner * share + p * piece, piece)
            picked[i * piece:(i + 1) * piece] = comb_ref[pl.ds(at, piece), :]

        def some_columns(k, carry):
            some = pl.ds(pl.multiple_of(k * step_cols, step_cols), step_cols)
            out[:, some] = jnp.dot(
                picked[...], pg[:, some], preferred_element_type=jnp.float32
            )
            return carry

        lax.fori_loop(0, hid // step_cols, some_columns, 0)

    def pair_copy(p):
        return pltpu.make_async_remote_copy(
            src_ref=pair_out.at[p], dst_ref=pair_in.at[p],
            send_sem=pair_sem.at[p, 0], recv_sem=pair_sem.at[p, 1],
            device_id={"feat": sibling}, device_id_type=MESH,
        )

    def chip_copy(p, i):
        return pltpu.make_async_remote_copy(
            src_ref=chip_out.at[p, i - 1], dst_ref=chip_in.at[p, i - 1],
            send_sem=chip_ssem.at[p, i - 1], recv_sem=chip_rsem.at[p, i - 1],
            device_id={"feat": chip_at(i)}, device_id_type=MESH,
        )

    def z_copy(p, i):
        return pltpu.make_async_remote_copy(
            src_ref=z_out.at[p, i - 1], dst_ref=z_in.at[p, i - 1],
            send_sem=z_ssem.at[p, i - 1], recv_sem=z_rsem.at[p, i - 1],
            device_id={"grp": z_at(i)}, device_id_type=MESH,
        )

    def g_copy(p, i):
        return pltpu.make_async_remote_copy(
            src_ref=g_out.at[p], dst_ref=g_in.at[p, i - 1],
            send_sem=g_ssem.at[p, i - 1], recv_sem=g_rsem.at[p, i - 1],
            device_id={"grp": z_at(i)}, device_id_type=MESH,
        )

    def columns(z):
        return pl.ds(pl.multiple_of(z * cw, cw), cw)

    def pair_stage(p):
        terms(p, 1 - core, pair_out.at[p])
        pair_copy(p).start()

    def chip_stage(p):
        terms(p, core, mine)
        pair_copy(p).wait_recv()
        own[p] = mine[:piece] + pair_in[p, :piece]
        for i in range(1, nc):
            part = pl.ds(i * piece, piece)
            chip_out[p, i - 1] = (mine[part] + pair_in[p, part]).astype(jnp.bfloat16)
            chip_copy(p, i).start()

    def z_stage(p):
        total = own[p]
        for i in range(1, nc):
            chip_copy(p, i).wait_recv()
            total = total + chip_in[p, i - 1].astype(jnp.float32)
        red[p] = total
        for i in range(1, nz):
            z_out[p, i - 1] = red[p, :, columns(z_at(i))].astype(jnp.bfloat16)
            z_copy(p, i).start()

    def g_stage(p):
        total = red[p, :, columns(mz)]
        for i in range(1, nz):
            z_copy(p, i).wait_recv()
            total = total + z_in[p, i - 1].astype(jnp.float32)
        g_out[p] = total.astype(jnp.bfloat16)
        for i in range(1, nz):
            g_copy(p, i).start()
        grad_ref[pl.ds(p * piece, piece), columns(mz)] = g_out[p].astype(jnp.float32)

    def last_stage(p):
        for i in range(1, nz):
            g_copy(p, i).wait_recv()
            grad_ref[pl.ds(p * piece, piece), columns(lax.rem(mz - i + nz, nz))] = (
                g_in[p, i - 1].astype(jnp.float32)
            )

    pair_stage(0)
    pair_stage(1)
    chip_stage(0)
    pair_stage(2)
    chip_stage(1)
    chip_stage(2)
    z_stage(0)
    z_stage(1)
    g_stage(0)
    z_stage(2)
    g_stage(1)
    g_stage(2)
    for p in range(PIECES):
        last_stage(p)
    for p in range(PIECES):
        pair_copy(p).wait_send()
        for i in range(1, nc):
            chip_copy(p, i).wait_send()
        for i in range(1, nz):
            z_copy(p, i).wait_send()
            g_copy(p, i).wait_send()


def per_device(
    n, nz,
    features, adj_tiles, tile_rows, tile_cols, self_blocks, weight, proj_bias, cotangent,
):
    feats = features[0]
    width, side = feats.shape[1], feats.shape[2]
    tiles = adj_tiles.shape[1]
    block_count = self_blocks.shape[1]
    rows = block_count // n
    depth, hid = weight.shape
    nodes = rows * side
    share = depth // n
    piece = share // PIECES
    nc = n // 2
    cw = hid // nz

    row_of = tile_rows[0]
    keep = jnp.concatenate(
        [jnp.zeros((1,), jnp.float32), (row_of[1:] == row_of[:-1]).astype(jnp.float32)]
    )
    last = jnp.sum(
        (row_of[None, :] <= jnp.arange(block_count, dtype=jnp.int32)[:, None]).astype(jnp.int32),
        axis=1,
    ) - 1

    smem = pl.BlockSpec(memory_space=pltpu.SMEM)
    vmem = pl.BlockSpec(memory_space=pltpu.VMEM)
    combined = pl.pallas_call(
        functools.partial(exchange_kernel, n),
        out_shape=jax.ShapeDtypeStruct((depth, nodes), jnp.bfloat16),
        in_specs=[smem] * 4 + [vmem] * 2,
        out_specs=vmem,
        scratch_shapes=[
            pltpu.VMEM((n, 2, rows, width, side), jnp.bfloat16),
            pltpu.VMEM((n, 2, rows, width, side), jnp.bfloat16),
            pltpu.VMEM((tiles, width, side), jnp.float32),
            pltpu.SemaphoreType.DMA((n, 2)),
            pltpu.SemaphoreType.DMA((n, 2)),
        ],
        compiler_params=pltpu.CompilerParams(
            collective_id=0, has_side_effects=True, vmem_limit_bytes=VMEM_BYTES
        ),
        name="exchange",
    )(tile_cols[0], keep, last, self_blocks[0], feats, adj_tiles[0])

    dma = pltpu.SemaphoreType.DMA
    hidden, weight_grad = pl.pallas_call(
        functools.partial(layer_kernel, n, nz),
        out_shape=(
            jax.ShapeDtypeStruct((nodes, hid), jnp.bfloat16),
            jax.ShapeDtypeStruct((share, hid), jnp.float32),
        ),
        in_specs=[vmem] * 4,
        out_specs=(vmem, vmem),
        scratch_shapes=[
            pltpu.VMEM((nodes, hid), jnp.bfloat16),
            pltpu.VMEM((256, depth), jnp.bfloat16),
            pltpu.VMEM((nc * piece, nodes), jnp.bfloat16),
            pltpu.VMEM((nc * piece, hid), jnp.float32),
            pltpu.VMEM((PIECES, nc * piece, hid), jnp.float32),
            pltpu.VMEM((PIECES, nc * piece, hid), jnp.float32),
            pltpu.VMEM((PIECES, piece, hid), jnp.float32),
            pltpu.VMEM((PIECES, nc - 1, piece, hid), jnp.bfloat16),
            pltpu.VMEM((PIECES, nc - 1, piece, hid), jnp.bfloat16),
            pltpu.VMEM((PIECES, piece, hid), jnp.float32),
            pltpu.VMEM((PIECES, nz - 1, piece, cw), jnp.bfloat16),
            pltpu.VMEM((PIECES, nz - 1, piece, cw), jnp.bfloat16),
            pltpu.VMEM((PIECES, piece, cw), jnp.bfloat16),
            pltpu.VMEM((PIECES, nz - 1, piece, cw), jnp.bfloat16),
            dma((PIECES, 2)),
            dma((PIECES, nc - 1)),
            dma((PIECES, nc - 1)),
            dma((PIECES, nz - 1)),
            dma((PIECES, nz - 1)),
            dma((PIECES, nz - 1)),
            dma((PIECES, nz - 1)),
        ],
        compiler_params=pltpu.CompilerParams(
            collective_id=1, has_side_effects=True, vmem_limit_bytes=VMEM_BYTES
        ),
        name="layer",
    )(combined, weight, proj_bias[None], cotangent[0])
    return (hidden[None], weight_grad)


def solution(mesh):
    return jax.shard_map(
        functools.partial(per_device, mesh.shape["feat"], mesh.shape["grp"]),
        mesh=mesh,
        in_specs=(
            P("grp", None, "feat", None),
            P("grp", None, None, None),
            P("grp", None),
            P("grp", None),
            P("grp", None),
            P(),
            P(),
            P("grp", "feat", None),
        ),
        out_specs=(P("grp", "feat", None), P("feat", None)),
        check_vma=False,
    )
```

time: 260 us -> 101 us (0.39)
  waiting for transfers between devices: 155 us -> 0 us
  Pallas kernels: 0 us -> 93.6 us
  blocking collectives: 42.8 us -> 0 us
  matrix products: 23.6 us -> 0 us
  local copies, waits for them, and re-layouts: 19.7 us -> 4.04 us
  between operations: 14.1 us -> 0.66 us
    psum x1 -> x0, waiting for transfers between devices: 155 us -> none  [per_device(): totals = lax.psum(partial_grad, ('grp', 'feat'))]
    pallas_call x0 -> x2, Pallas kernels: none -> 93.6 us  [the longest x1 50.1 us: per_device(): pl.pallas_call(functools.partial(layer_kernel, n, nz), out_shape=(jax.Sha...]
    all_to_all x1 -> x0, blocking collectives: 42.8 us -> none  [per_device(): lax.all_to_all(stacked, 'feat', split_axis=0, concat_axis=2, tiled=True)]
    dot_general x4 -> x0, matrix products: 23.6 us -> none  [the longest x1 8.52 us: per_device(): jnp.einsum('rcd,ch->rdh', combined, weight, preferred_element_type=jnp.fl...]
    gather x2 -> x0, local copies, waits for them, and re-layouts: 8.9 us -> none  [the longest x1 4.67 us: per_device(): picked = jnp.take(local_blocks, tile_cols[0], axis=0)]
    dot_general x1 -> x0, local copies, waits for them, and re-layouts: 4.65 us -> none  [per_device(): jnp.einsum('rcd,ch->rdh', combined, weight, preferred_element_type=jnp.fl...]
    unnamed x10 -> x4, local copies, waits for them, and re-layouts: 0.03 us -> 4.04 us
  transfers between devices with their start and end apart: 1 -> 0, of which waited for: 1 -> 0; matrix products, arithmetic and copies ran while one was open for 0% -> 0% of each run, Pallas kernels for 0% -> 0%
where the time goes in v1:
time: 101 us
  Pallas kernels  93.6 us (93%)
  local copies, waits for them, and re-layouts  4.04 us (4%)
  other arithmetic  2.68 us (3%)
    pallas_call x1, Pallas kernels, per_device(): pl.pallas_call(functools.partial(layer_kernel, n, nz), out_shape=(jax.Sha...  50.1 us
    pallas_call x1, Pallas kernels, per_device(): pl.pallas_call(functools.partial(exchange_kernel, n), out_shape=jax.Shape...  43.5 us
    unnamed x4, local copies, waits for them, and re-layouts  4.04 us

profile of v1, /device:TPU:0, one launch (start us, length us, event | category | flops | bytes accessed | tf_op | source)
XLA Modules:
  0.0 101.0 jit_solution(5033879746117176588)
XLA Ops:
  0.6 0.8 convert_reduce_fusion
  1.4 0.5 broadcast_add_fusion.last_ref
  1.9 0.8 compare_bitcast_fusion
  2.7 0.6 add_convert_fusion.keep_ref
  3.3 43.5 %exchange.1.comb_ref = bf16[1536,1024]{1,0:T(8,128)(2,1)} custom-call(s32[96]{0:T(128)} %bitcast.15, f32[96]{0:T(128)} %add_convert_fusion.keep_ref, s32[64]{0:T(128)} %broadcast_add_fusion.last_ref, s32[64]{0:T(128)} %bitcast.16, bf16[192,96,128]{2,1,0:T(8,128)(2,1)} %bitcast.10, bf16[96,128,128]{2,1,0:T(8,128)(2,1)} %bitcast.11), custom_call_target="tpu_custom_call" | custom-call | tf_op jit(solution)/shard_map/exchange/pallas_call | solution.py:315
  46.9 50.1 %layer.1 = (bf16[1024,1024]{1,0:T(8,128)(2,1)}, f32[192,1024]{1,0:T(8,128)}) custom-call(bf16[1536,1024]{1,0:T(8,128)(2,1)} %exchange.1.comb_ref, bf16[1536,1024]{1,0:T(8,128)(2,1)} %w_ref.1, f32[1,1024]{1,0:T(1,128)} %bitcast.14, bf16[1024,1024]{1,0:T(8,128)(2,1)} %bitcast.13), custom_call_target="tpu_custom_call" | custom-call | tf_op jit(solution)/shard_map/layer/pallas_call | solution.py:334
  96.9 0.0 copy-start
  96.9 3.2 %copy.12 = bf16[1,1024,1024]{2,1,0:T(8,128)(2,1)} copy(bf16[1,1024,1024]{2,1,0:T(8,128)(2,1)} %bitcast.12) | data formatting | bytes 4194304
  100.1 0.0 copy-done
  100.1 0.9 copy.13
Async XLA Ops:
  96.9 3.2 %copy-start = (f32[192,1024]{1,0:T(8,128)S(1)}, f32[192,1024]{1,0:T(8,128)}, u32[]{:S(2)}) copy-start(f32[192,1024]{1,0:T(8,128)} %get-tuple-element.9) | copy-start | bytes 2359300

commit v2 on v1

v2 whole, which is shorter than its diff:
```python
import functools

import jax
import jax.numpy as jnp
from jax import lax
from jax.experimental import pallas as pl
from jax.experimental.pallas import tpu as pltpu
from jax.sharding import PartitionSpec as P

MESH = pl.DeviceIdType.MESH
PIECES = 3
GROUP = 2
VMEM_BYTES = 60 * 1024 * 1024


def layer_kernel(
    n, nz, rows_ref, cols_ref, blocks_ref, feat_hbm, adj_hbm, w_hbm, bias_ref, cot_hbm,
    hid_hbm, grad_ref,
    feat, adj, w, cot, hidden, sendbuf, recvbuf, scan, last, comb_ref,
    pg, lhs, picked, mine, pair_out, pair_in, own, chip_out, chip_in, red,
    z_out, z_in, g_out, g_in,
    load_sem, hid_sem, send_sem, recv_sem,
    pair_sem, chip_ssem, chip_rsem, z_ssem, z_rsem, g_ssem, g_rsem,
):
    me = lax.axis_index("feat")
    mz = lax.axis_index("grp")
    nc = n // 2
    chip, core = me // 2, lax.rem(me, 2)
    sibling = chip * 2 + (1 - core)
    share, hid = grad_ref.shape
    piece = share // PIECES
    cw = hid // nz
    rows = sendbuf.shape[2]
    width = feat.shape[1]
    tiles = adj.shape[0]
    groups = rows // GROUP
    step_nodes = GROUP * 128
    step_cols = 256

    def chip_at(i):
        return lax.rem(chip + i, nc) * 2 + core

    def z_at(i):
        return lax.rem(mz + i, nz)

    loads = [
        pltpu.make_async_copy(src, dst, load_sem.at[k])
        for k, (src, dst) in enumerate(
            [(feat_hbm, feat), (adj_hbm, adj), (w_hbm, w), (cot_hbm, cot)]
        )
    ]
    for load in loads:
        load.start()

    barrier = pltpu.get_barrier_semaphore()

    def greet(i, carry):
        pl.semaphore_signal(
            barrier, inc=1, device_id={"feat": lax.rem(me + i, n)}, device_id_type=MESH
        )
        return carry

    lax.fori_loop(1, n, greet, 0)
    for i in range(1, nz):
        pl.semaphore_signal(barrier, inc=1, device_id={"grp": z_at(i)}, device_id_type=MESH)

    def fill_self(i, carry):
        peer = lax.rem(me + i, n)
        for r in range(rows):
            sendbuf[i, 0, r] = feat[blocks_ref[peer * rows + r]]
        return carry

    def self_copy(i, src):
        return pltpu.make_async_remote_copy(
            src_ref=sendbuf.at[i, 0],
            dst_ref=recvbuf.at[src, 0],
            send_sem=send_sem.at[i, 0],
            recv_sem=recv_sem.at[src, 0],
            device_id={"feat": lax.rem(me + i, n)},
            device_id_type=MESH,
        )

    def agg_copy(i, q, src):
        some = pl.ds(q * GROUP, GROUP)
        return pltpu.make_async_remote_copy(
            src_ref=sendbuf.at[i, 1, some],
            dst_ref=recvbuf.at[src, 1, some],
            send_sem=send_sem.at[i, 1 + q],
            recv_sem=recv_sem.at[src, 1 + q],
            device_id={"feat": lax.rem(me + i, n)},
            device_id_type=MESH,
        )

    def send_self(i, carry):
        fill_self(i, carry)
        self_copy(i, me).start()
        return carry

    loads[0].wait()
    fill_self(1, 0)
    pl.semaphore_wait(barrier, (n - 1) + (nz - 1))
    self_copy(1, me).start()
    lax.fori_loop(2, n, send_self, 0)
    for r in range(rows):
        recvbuf[me, 0, r] = feat[blocks_ref[me * rows + r]]

    loads[1].wait()

    def tile_terms(step, carry):
        for k in range(8):
            t = step * 8 + k
            scan[t] = lax.dot_general(
                feat[cols_ref[t]], adj[t], (((1,), (1,)), ((), ())),
                preferred_element_type=jnp.float32,
            )
        return carry

    lax.fori_loop(0, tiles // 8, tile_terms, 0)

    def running_sums(step, acc):
        for k in range(8):
            t = step * 8 + k
            same = rows_ref[t] == rows_ref[jnp.maximum(t - 1, 0)]
            acc = scan[t] + jnp.where(same, 1.0, 0.0) * acc
            scan[t] = acc
        return acc

    lax.fori_loop(0, tiles // 8, running_sums, jnp.zeros((width, 128), jnp.float32))

    def find_last(r, carry):
        at = jnp.int32(0)
        step = 1 << (tiles.bit_length() - 1)
        while step:
            there = at + step
            fits = (there < tiles) & (rows_ref[jnp.minimum(there, tiles - 1)] <= r)
            at = jnp.where(fits, there, at)
            step //= 2
        last[r] = at
        return carry

    lax.fori_loop(0, n * rows, find_last, 0)

    def send_group(q, carry):
        def send_agg(i, inner):
            peer = lax.rem(me + i, n)
            for k in range(GROUP):
                r = q * GROUP + k
                sendbuf[i, 1, r] = scan[last[peer * rows + r]].astype(jnp.bfloat16)
            agg_copy(i, q, me).start()
            return inner

        return lax.fori_loop(1, n, send_agg, carry)

    lax.fori_loop(0, groups, send_group, 0)
    for r in range(rows):
        recvbuf[me, 1, r] = scan[last[me * rows + r]].astype(jnp.bfloat16)

    loads[2].wait()
    loads[3].wait()

    def wait_self(i, carry):
        self_copy(i, lax.rem(me - i + n, n)).wait_recv()
        return carry

    lax.fori_loop(1, n, wait_self, 0)

    def hid_copy(q):
        at = pl.ds(pl.multiple_of(q * step_nodes, step_nodes), step_nodes)
        return pltpu.make_async_copy(hidden.at[at], hid_hbm.at[at], hid_sem.at[q])

    def forward(q, carry):
        def wait_agg(i, inner):
            agg_copy(i, q, lax.rem(me - i + n, n)).wait_recv()
            return inner

        lax.fori_loop(1, n, wait_agg, 0)
        for kind in range(2):
            base = kind * n * width
            for k in range(GROUP):
                r = q * GROUP + k
                lanes = pl.ds(pl.multiple_of(r * 128, 128), 128)
                if width % 16 == 0:
                    for src in range(n):
                        comb_ref[pl.ds(base + src * width, width), lanes] = recvbuf[src, kind, r]
                else:
                    whole = jnp.concatenate(
                        [recvbuf[src, kind, r].astype(jnp.float32) for src in range(n)], axis=0
                    )
                    comb_ref[pl.ds(base, n * width), lanes] = whole.astype(jnp.bfloat16)

        at = pl.ds(pl.multiple_of(q * step_nodes, step_nodes), step_nodes)
        lhs[...] = comb_ref[:, at].T

        def forward_columns(k, inner):
            some = pl.ds(pl.multiple_of(k * step_cols, step_cols), step_cols)
            pre = jnp.dot(lhs[...], w[:, some], preferred_element_type=jnp.float32)
            pre = pre + bias_ref[:, some]
            decay = jnp.exp(jnp.minimum(pre, 0.0))
            hidden[at, some] = jnp.where(pre > 0, pre, decay - 1.0).astype(jnp.bfloat16)
            pg[at, some] = (cot[at, some].astype(jnp.float32) * decay).astype(jnp.bfloat16)
            return inner

        lax.fori_loop(0, hid // step_cols, forward_columns, 0)
        hid_copy(q).start()
        return carry

    lax.fori_loop(0, groups, forward, 0)

    def terms(p, parity, out):
        for i in range(nc):
            owner = lax.rem(chip + i, nc) * 2 + parity
            at = pl.multiple_of(owner * share + p * piece, piece)
            picked[i * piece:(i + 1) * piece] = comb_ref[pl.ds(at, piece), :]

        def some_columns(k, carry):
            some = pl.ds(pl.multiple_of(k * step_cols, step_cols), step_cols)
            out[:, some] = jnp.dot(
                picked[...], pg[:, some], preferred_element_type=jnp.float32
            )
            return carry

        lax.fori_loop(0, hid // step_cols, some_columns, 0)

    def pair_copy(p):
        return pltpu.make_async_remote_copy(
            src_ref=pair_out.at[p], dst_ref=pair_in.at[p],
            send_sem=pair_sem.at[p, 0], recv_sem=pair_sem.at[p, 1],
            device_id={"feat": sibling}, device_id_type=MESH,
        )

    def chip_copy(p, i):
        return pltpu.make_async_remote_copy(
            src_ref=chip_out.at[p, i - 1], dst_ref=chip_in.at[p, i - 1],
            send_sem=chip_ssem.at[p, i - 1], recv_sem=chip_rsem.at[p, i - 1],
            device_id={"feat": chip_at(i)}, device_id_type=MESH,
        )

    def z_copy(p, i):
        return pltpu.make_async_remote_copy(
            src_ref=z_out.at[p, i - 1], dst_ref=z_in.at[p, i - 1],
            send_sem=z_ssem.at[p, i - 1], recv_sem=z_rsem.at[p, i - 1],
            device_id={"grp": z_at(i)}, device_id_type=MESH,
        )

    def g_copy(p, i):
        return pltpu.make_async_remote_copy(
            src_ref=g_out.at[p], dst_ref=g_in.at[p, i - 1],
            send_sem=g_ssem.at[p, i - 1], recv_sem=g_rsem.at[p, i - 1],
            device_id={"grp": z_at(i)}, device_id_type=MESH,
        )

    def columns(z):
        return pl.ds(pl.multiple_of(z * cw, cw), cw)

    def pair_stage(p):
        terms(p, 1 - core, pair_out.at[p])
        pair_copy(p).start()

    def chip_stage(p):
        terms(p, core, mine)
        pair_copy(p).wait_recv()
        own[p] = mine[:piece] + pair_in[p, :piece]
        for i in range(1, nc):
            part = pl.ds(i * piece, piece)
            chip_out[p, i - 1] = (mine[part] + pair_in[p, part]).astype(jnp.bfloat16)
            chip_copy(p, i).start()

    def z_stage(p):
        total = own[p]
        for i in range(1, nc):
            chip_copy(p, i).wait_recv()
            total = total + chip_in[p, i - 1].astype(jnp.float32)
        red[p] = total
        for i in range(1, nz):
            z_out[p, i - 1] = red[p, :, columns(z_at(i))].astype(jnp.bfloat16)
            z_copy(p, i).start()

    def g_stage(p):
        total = red[p, :, columns(mz)]
        for i in range(1, nz):
            z_copy(p, i).wait_recv()
            total = total + z_in[p, i - 1].astype(jnp.float32)
        g_out[p] = total.astype(jnp.bfloat16)
        for i in range(1, nz):
            g_copy(p, i).start()
        grad_ref[pl.ds(p * piece, piece), columns(mz)] = g_out[p]

    def last_stage(p):
        for i in range(1, nz):
            g_copy(p, i).wait_recv()
            grad_ref[pl.ds(p * piece, piece), columns(lax.rem(mz - i + nz, nz))] = g_in[p, i - 1]

    pair_stage(0)
    pair_stage(1)
    chip_stage(0)
    pair_stage(2)
    chip_stage(1)
    chip_stage(2)
    z_stage(0)
    z_stage(1)
    g_stage(0)
    z_stage(2)
    g_stage(1)
    g_stage(2)
    for p in range(PIECES):
        last_stage(p)
    for p in range(PIECES):
        pair_copy(p).wait_send()
        for i in range(1, nc):
            chip_copy(p, i).wait_send()
        for i in range(1, nz):
            z_copy(p, i).wait_send()
            g_copy(p, i).wait_send()

    def wait_out(i, carry):
        self_copy(i, me).wait_send()
        for q in range(groups):
            agg_copy(i, q, me).wait_send()
        return carry

    lax.fori_loop(1, n, wait_out, 0)
    for q in range(groups):
        hid_copy(q).wait()


def per_device(
    n, nz,
    features, adj_tiles, tile_rows, tile_cols, self_blocks, weight, proj_bias, cotangent,
):
    feats, adj = features[0], adj_tiles[0]
    width, side = feats.shape[1], feats.shape[2]
    tiles = adj.shape[0]
    block_count = self_blocks.shape[1]
    rows = block_count // n
    depth, hid = weight.shape
    nodes = rows * side
    share = depth // n
    piece = share // PIECES
    nc = n // 2
    cw = hid // nz
    groups = rows // GROUP
    step_nodes = GROUP * side

    smem = pl.BlockSpec(memory_space=pltpu.SMEM)
    vmem = pl.BlockSpec(memory_space=pltpu.VMEM)
    anywhere = pl.BlockSpec(memory_space=pl.ANY)
    dma = pltpu.SemaphoreType.DMA
    hidden, weight_grad = pl.pallas_call(
        functools.partial(layer_kernel, n, nz),
        out_shape=(
            jax.ShapeDtypeStruct((nodes, hid), jnp.bfloat16),
            jax.ShapeDtypeStruct((share, hid), jnp.bfloat16),
        ),
        in_specs=[smem] * 3 + [anywhere] * 3 + [vmem, anywhere],
        out_specs=(anywhere, vmem),
        scratch_shapes=[
            pltpu.VMEM(feats.shape, jnp.bfloat16),
            pltpu.VMEM(adj.shape, jnp.bfloat16),
            pltpu.VMEM(weight.shape, jnp.bfloat16),
            pltpu.VMEM((nodes, hid), jnp.bfloat16),
            pltpu.VMEM((nodes, hid), jnp.bfloat16),
            pltpu.VMEM((n, 2, rows, width, side), jnp.bfloat16),
            pltpu.VMEM((n, 2, rows, width, side), jnp.bfloat16),
            pltpu.VMEM((tiles, width, side), jnp.float32),
            pltpu.SMEM((block_count,), jnp.int32),
            pltpu.VMEM((depth, nodes), jnp.bfloat16),
            pltpu.VMEM((nodes, hid), jnp.bfloat16),
            pltpu.VMEM((step_nodes, depth), jnp.bfloat16),
            pltpu.VMEM((nc * piece, nodes), jnp.bfloat16),
            pltpu.VMEM((nc * piece, hid), jnp.float32),
            pltpu.VMEM((PIECES, nc * piece, hid), jnp.float32),
            pltpu.VMEM((PIECES, nc * piece, hid), jnp.float32),
            pltpu.VMEM((PIECES, piece, hid), jnp.float32),
            pltpu.VMEM((PIECES, nc - 1, piece, hid), jnp.bfloat16),
            pltpu.VMEM((PIECES, nc - 1, piece, hid), jnp.bfloat16),
            pltpu.VMEM((PIECES, piece, hid), jnp.float32),
            pltpu.VMEM((PIECES, nz - 1, piece, cw), jnp.bfloat16),
            pltpu.VMEM((PIECES, nz - 1, piece, cw), jnp.bfloat16),
            pltpu.VMEM((PIECES, piece, cw), jnp.bfloat16),
            pltpu.VMEM((PIECES, nz - 1, piece, cw), jnp.bfloat16),
            dma((4,)),
            dma((groups,)),
            dma((n, 1 + groups)),
            dma((n, 1 + groups)),
            dma((PIECES, 2)),
            dma((PIECES, nc - 1)),
            dma((PIECES, nc - 1)),
            dma((PIECES, nz - 1)),
            dma((PIECES, nz - 1)),
            dma((PIECES, nz - 1)),
            dma((PIECES, nz - 1)),
        ],
        compiler_params=pltpu.CompilerParams(
            collective_id=0, has_side_effects=True, vmem_limit_bytes=VMEM_BYTES
        ),
        name="layer",
    )(
        tile_rows[0], tile_cols[0], self_blocks[0], feats, adj, weight, proj_bias[None],
        cotangent[0],
    )
    return (hidden[None], weight_grad.astype(jnp.float32))


def solution(mesh):
    return jax.shard_map(
        functools.partial(per_device, mesh.shape["feat"], mesh.shape["grp"]),
        mesh=mesh,
        in_specs=(
            P("grp", None, "feat", None),
            P("grp", None, None, None),
            P("grp", None),
            P("grp", None),
            P("grp", None),
            P(),
            P(),
            P("grp", "feat", None),
        ),
        out_specs=(P("grp", "feat", None), P("feat", None)),
        check_vma=False,
    )
```

time: 101 us -> 85.6 us (0.85)
  Pallas kernels: 93.6 us -> 79.7 us
    pallas_call x1 -> x0, Pallas kernels: 43.5 us -> none  [per_device(): pl.pallas_call(functools.partial(exchange_kernel, n), out_shape=jax.Shape...]
    pallas_call x1, Pallas kernels: 50.1 us -> 79.7 us  [per_device(): pl.pallas_call(functools.partial(layer_kernel, n, nz), out_shape=(jax.Sha...]
    convert_element_type x1, other arithmetic: 0.8 us -> 1.96 us  [per_device(): return (hidden[None], weight_grad.astype(jnp.float32))]
    unnamed x4 -> x1, local copies, waits for them, and re-layouts: 4.04 us -> 3.08 us
where the time goes in v2:
time: 85.6 us; the launch traced here: 85.4 us
  Pallas kernels  79.7 us (93%)
  local copies, waits for them, and re-layouts  3.08 us (4%)
  other arithmetic  1.96 us (2%)
    pallas_call x1, Pallas kernels, per_device(): pl.pallas_call(functools.partial(layer_kernel, n, nz), out_shape=(jax.Sha...  79.7 us
    unnamed x1, local copies, waits for them, and re-layouts  3.08 us
    convert_element_type x1, other arithmetic, per_device(): return (hidden[None], weight_grad.astype(jnp.float32))  1.96 us

profile of v2, /device:TPU:0, one launch (start us, length us, event | category | flops | bytes accessed | tf_op | source)
XLA Modules:
  0.0 85.4 jit_solution(13168401278239283812)
XLA Ops:
  0.6 79.7 %layer.1 = (bf16[1024,1024]{1,0:T(8,128)(2,1)}, bf16[192,1024]{1,0:T(8,128)(2,1)}) custom-call(s32[96]{0:T(128)} %bitcast.13, s32[96]{0:T(128)} %bitcast.14, s32[64]{0:T(128)} %bitcast.15, bf16[192,96,128]{2,1,0:T(8,128)(2,1)} %bitcast.8, bf16[96,128,128]{2,1,0:T(8,128)(2,1)} %bitcast.9, bf16[1536,1024]{1,0:T(8,128)(2,1)} %w_hbm.1, f32[1,1024]{1,0:T(1,128)} %bitcast.12, ...), custom_call_target="tpu_custom_call" | custom-call | tf_op jit(solution)/shard_map/layer/pallas_call | solution.py:348
  80.4 2.0 %convert_element_type.3 = f32[192,1024]{1,0:T(8,128)} convert(bf16[192,1024]{1,0:T(8,128)(2,1)} %get-tuple-element.5) | non-fusion elementwise | flops 196608 | bytes 1179648 | tf_op jit(solution)/shard_map/convert_element_type | solution.py:401
  82.3 3.1 %copy.11 = bf16[1,1024,1024]{2,1,0:T(8,128)(2,1)} copy(bf16[1,1024,1024]{2,1,0:T(8,128)(2,1)} %bitcast.11) | data formatting | bytes 4194304

commit v3 on v2

--- a/solution.py
+++ b/solution.py
@@ -1,4 +1,5 @@
 import functools
+import math
 
 import jax
 import jax.numpy as jnp
@@ -17,10 +18,10 @@
     n, nz, rows_ref, cols_ref, blocks_ref, feat_hbm, adj_hbm, w_hbm, bias_ref, cot_hbm,
     hid_hbm, grad_ref,
     feat, adj, w, cot, hidden, sendbuf, recvbuf, scan, last, comb_ref,
-    pg, lhs, picked, mine, pair_out, pair_in, own, chip_out, chip_in, red,
+    pg, lhs, picked, mine, pair_out, pair_in, own, one_out, one_in, two_out, two_in, red,
     z_out, z_in, g_out, g_in,
     load_sem, hid_sem, send_sem, recv_sem,
-    pair_sem, chip_ssem, chip_rsem, z_ssem, z_rsem, g_ssem, g_rsem,
+    pair_sem, one_ssem, one_rsem, two_ssem, two_rsem, z_ssem, z_rsem, g_ssem, g_rsem,
 ):
     me = lax.axis_index("feat")
     mz = lax.axis_index("grp")
@@ -29,6 +30,10 @@
     sibling = chip * 2 + (1 - core)
     share, hid = grad_ref.shape
     piece = share // PIECES
+    part = one_out.shape[3]
+    parts = piece // part
+    count = PIECES * parts
+    side = one_out.shape[2]
     cw = hid // nz
     rows = sendbuf.shape[2]
     width = feat.shape[1]
@@ -37,8 +42,8 @@
     step_nodes = GROUP * 128
     step_cols = 256
 
-    def chip_at(i):
-        return lax.rem(chip + i, nc) * 2 + core
+    def chip_at(outer, inner):
+        return lax.rem(chip // side + outer, side) * side + lax.rem(chip + inner, side)
 
     def z_at(i):
         return lax.rem(mz + i, nz)
@@ -49,8 +54,7 @@
             [(feat_hbm, feat), (adj_hbm, adj), (w_hbm, w), (cot_hbm, cot)]
         )
     ]
-    for load in loads:
-        load.start()
+    loads[0].start()
 
     barrier = pltpu.get_barrier_semaphore()
 
@@ -97,6 +101,8 @@
         return carry
 
     loads[0].wait()
+    for load in loads[1:]:
+        load.start()
     fill_self(1, 0)
     pl.semaphore_wait(barrier, (n - 1) + (nz - 1))
     self_copy(1, me).start()
@@ -208,7 +214,7 @@
 
     def terms(p, parity, out):
         for i in range(nc):
-            owner = lax.rem(chip + i, nc) * 2 + parity
+            owner = chip_at(i // side, i % side) * 2 + parity
             at = pl.multiple_of(owner * share + p * piece, piece)
             picked[i * piece:(i + 1) * piece] = comb_ref[pl.ds(at, piece), :]
 
@@ -228,24 +234,37 @@
             device_id={"feat": sibling}, device_id_type=MESH,
         )
 
-    def chip_copy(p, i):
-        return pltpu.make_async_remote_copy(
-            src_ref=chip_out.at[p, i - 1], dst_ref=chip_in.at[p, i - 1],
-            send_sem=chip_ssem.at[p, i - 1], recv_sem=chip_rsem.at[p, i - 1],
-            device_id={"feat": chip_at(i)}, device_id_type=MESH,
-        )
-
-    def z_copy(p, i):
-        return pltpu.make_async_remote_copy(
-            src_ref=z_out.at[p, i - 1], dst_ref=z_in.at[p, i - 1],
-            send_sem=z_ssem.at[p, i - 1], recv_sem=z_rsem.at[p, i - 1],
+    def offsets(c, phase, i):
+        return (0, i) if (c + phase) % 2 == 0 else (i, 0)
+
+    def block_rows(c, outer, inner):
+        return pl.ds((outer * side + inner) * piece + (c % parts) * part, part)
+
+    def one_copy(c, i):
+        return pltpu.make_async_remote_copy(
+            src_ref=one_out.at[c, i - 1], dst_ref=one_in.at[c, i - 1],
+            send_sem=one_ssem.at[c, i - 1], recv_sem=one_rsem.at[c, i - 1],
+            device_id={"feat": chip_at(*offsets(c, 0, i)) * 2 + core}, device_id_type=MESH,
+        )
+
+    def two_copy(c, i):
+        return pltpu.make_async_remote_copy(
+            src_ref=two_out.at[c, i - 1], dst_ref=two_in.at[c, i - 1],
+            send_sem=two_ssem.at[c, i - 1], recv_sem=two_rsem.at[c, i - 1],
+            device_id={"feat": chip_at(*offsets(c, 1, i)) * 2 + core}, device_id_type=MESH,
+        )
+
+    def z_copy(c, i):
+        return pltpu.make_async_remote_copy(
+            src_ref=z_out.at[c, i - 1], dst_ref=z_in.at[c, i - 1],
+            send_sem=z_ssem.at[c, i - 1], recv_sem=z_rsem.at[c, i - 1],
             device_id={"grp": z_at(i)}, device_id_type=MESH,
         )
 
-    def g_copy(p, i):
-        return pltpu.make_async_remote_copy(
-            src_ref=g_out.at[p], dst_ref=g_in.at[p, i - 1],
-            send_sem=g_ssem.at[p, i - 1], recv_sem=g_rsem.at[p, i - 1],
+    def g_copy(c, i):
+        return pltpu.make_async_remote_copy(
+            src_ref=g_out.at[c], dst_ref=g_in.at[c, i - 1],
+            send_sem=g_ssem.at[c, i - 1], recv_sem=g_rsem.at[c, i - 1],
             device_id={"grp": z_at(i)}, device_id_type=MESH,
         )
 
@@ -256,61 +275,83 @@
         terms(p, 1 - core, pair_out.at[p])
         pair_copy(p).start()
 
-    def chip_stage(p):
-        terms(p, core, mine)
+    def one_stage(p):
+        terms(p, core, mine.at[p])
         pair_copy(p).wait_recv()
-        own[p] = mine[:piece] + pair_in[p, :piece]
-        for i in range(1, nc):
-            part = pl.ds(i * piece, piece)
-            chip_out[p, i - 1] = (mine[part] + pair_in[p, part]).astype(jnp.bfloat16)
-            chip_copy(p, i).start()
-
-    def z_stage(p):
-        total = own[p]
-        for i in range(1, nc):
-            chip_copy(p, i).wait_recv()
-            total = total + chip_in[p, i - 1].astype(jnp.float32)
-        red[p] = total
+        for c in range(p * parts, (p + 1) * parts):
+            for i in range(1, side):
+                for j in range(side):
+                    first, second = offsets(c, 0, i), offsets(c, 1, j)
+                    at = block_rows(c, first[0] + second[0], first[1] + second[1])
+                    one_out[c, i - 1, j] = (mine[p, at] + pair_in[p, at]).astype(jnp.bfloat16)
+                one_copy(c, i).start()
+
+    def two_stage(c):
+        p = c // parts
+        for i in range(1, side):
+            one_copy(c, i).wait_recv()
+        for j in list(range(1, side)) + [0]:
+            at = block_rows(c, *offsets(c, 1, j))
+            total = mine[p, at] + pair_in[p, at]
+            for i in range(1, side):
+                total = total + one_in[c, i - 1, j].astype(jnp.float32)
+            if j:
+                two_out[c, j - 1] = total.astype(jnp.bfloat16)
+                two_copy(c, j).start()
+            else:
+                own[c] = total
+
+    def z_stage(c):
+        total = own[c]
+        for i in range(1, side):
+            two_copy(c, i).wait_recv()
+            total = total + two_in[c, i - 1].astype(jnp.float32)
+        red[c] = total
         for i in range(1, nz):
-            z_out[p, i - 1] = red[p, :, columns(z_at(i))].astype(jnp.bfloat16)
-            z_copy(p, i).start()
-
-    def g_stage(p):
-        total = red[p, :, columns(mz)]
+            z_out[c, i - 1] = red[c, :, columns(z_at(i))].astype(jnp.bfloat16)
+            z_copy(c, i).start()
+
+    def g_stage(c):
+        total = red[c, :, columns(mz)]
         for i in range(1, nz):
-            z_copy(p, i).wait_recv()
-            total = total + z_in[p, i - 1].astype(jnp.float32)
-        g_out[p] = total.astype(jnp.bfloat16)
+            z_copy(c, i).wait_recv()
+            total = total + z_in[c, i - 1].astype(jnp.float32)
+        g_out[c] = total.astype(jnp.bfloat16)
         for i in range(1, nz):
-            g_copy(p, i).start()
-        grad_ref[pl.ds(p * piece, piece), columns(mz)] = g_out[p]
-
-    def last_stage(p):
+            g_copy(c, i).start()
+        grad_ref[pl.ds(c * part, part), columns(mz)] = g_out[c].astype(jnp.float32)
+
+    def last_stage(c):
         for i in range(1, nz):
-            g_copy(p, i).wait_recv()
-            grad_ref[pl.ds(p * piece, piece), columns(lax.rem(mz - i + nz, nz))] = g_in[p, i - 1]
+            g_copy(c, i).wait_recv()
+            grad_ref[pl.ds(c * part, part), columns(lax.rem(mz - i + nz, nz))] = (
+                g_in[c, i - 1].astype(jnp.float32)
+            )
 
     pair_stage(0)
     pair_stage(1)
-    chip_stage(0)
+    one_stage(0)
     pair_stage(2)
-    chip_stage(1)
-    chip_stage(2)
-    z_stage(0)
-    z_stage(1)
-    g_stage(0)
-    z_stage(2)
-    g_stage(1)
-    g_stage(2)
-    for p in range(PIECES):
-        last_stage(p)
+    one_stage(1)
+    two_stage(0)
+    one_stage(2)
+    for c in range(1, count + 2):
+        if c < count:
+            two_stage(c)
+        if c - 1 < count:
+            z_stage(c - 1)
+        g_stage(c - 2) if c >= 2 else None
+    for c in range(count):
+        last_stage(c)
     for p in range(PIECES):
         pair_copy(p).wait_send()
-        for i in range(1, nc):
-            chip_copy(p, i).wait_send()
+    for c in range(count):
+        for i in range(1, side):
+            one_copy(c, i).wait_send()
+            two_copy(c, i).wait_send()
         for i in range(1, nz):
-            z_copy(p, i).wait_send()
-            g_copy(p, i).wait_send()
+            z_copy(c, i).wait_send()
+            g_copy(c, i).wait_send()
 
     def wait_out(i, carry):
         self_copy(i, me).wait_send()
@@ -337,6 +378,9 @@
     share = depth // n
     piece = share // PIECES
     nc = n // 2
+    grid = math.isqrt(nc)
+    part = 32 if piece % 32 == 0 else piece
+    count = share // part
     cw = hid // nz
     groups = rows // GROUP
     step_nodes = GROUP * side
@@ -349,7 +393,7 @@
         functools.partial(layer_kernel, n, nz),
         out_shape=(
             jax.ShapeDtypeStruct((nodes, hid), jnp.bfloat16),
-            jax.ShapeDtypeStruct((share, hid), jnp.bfloat16),
+            jax.ShapeDtypeStruct((share, hid), jnp.float32),
         ),
         in_specs=[smem] * 3 + [anywhere] * 3 + [vmem, anywhere],
         out_specs=(anywhere, vmem),
@@ -367,28 +411,32 @@
             pltpu.VMEM((nodes, hid), jnp.bfloat16),
             pltpu.VMEM((step_nodes, depth), jnp.bfloat16),
             pltpu.VMEM((nc * piece, nodes), jnp.bfloat16),
-            pltpu.VMEM((nc * piece, hid), jnp.float32),
             pltpu.VMEM((PIECES, nc * piece, hid), jnp.float32),
             pltpu.VMEM((PIECES, nc * piece, hid), jnp.float32),
-            pltpu.VMEM((PIECES, piece, hid), jnp.float32),
-            pltpu.VMEM((PIECES, nc - 1, piece, hid), jnp.bfloat16),
-            pltpu.VMEM((PIECES, nc - 1, piece, hid), jnp.bfloat16),
-            pltpu.VMEM((PIECES, piece, hid), jnp.float32),
-            pltpu.VMEM((PIECES, nz - 1, piece, cw), jnp.bfloat16),
-            pltpu.VMEM((PIECES, nz - 1, piece, cw), jnp.bfloat16),
-            pltpu.VMEM((PIECES, piece, cw), jnp.bfloat16),
-            pltpu.VMEM((PIECES, nz - 1, piece, cw), jnp.bfloat16),
+            pltpu.VMEM((PIECES, nc * piece, hid), jnp.float32),
+            pltpu.VMEM((count, part, hid), jnp.float32),
+            pltpu.VMEM((count, grid - 1, grid, part, hid), jnp.bfloat16),
+            pltpu.VMEM((count, grid - 1, grid, part, hid), jnp.bfloat16),
+            pltpu.VMEM((count, grid - 1, part, hid), jnp.bfloat16),
+            pltpu.VMEM((count, grid - 1, part, hid), jnp.bfloat16),
+            pltpu.VMEM((count, part, hid), jnp.float32),
+            pltpu.VMEM((count, nz - 1, part, cw), jnp.bfloat16),
+            pltpu.VMEM((count, nz - 1, part, cw), jnp.bfloat16),
+            pltpu.VMEM((count, part, cw), jnp.bfloat16),
+            pltpu.VMEM((count, nz - 1, part, cw), jnp.bfloat16),
             dma((4,)),
             dma((groups,)),
             dma((n, 1 + groups)),
             dma((n, 1 + groups)),
             dma((PIECES, 2)),
-            dma((PIECES, nc - 1)),
-            dma((PIECES, nc - 1)),
-            dma((PIECES, nz - 1)),
-            dma((PIECES, nz - 1)),
-            dma((PIECES, nz - 1)),
-            dma((PIECES, nz - 1)),
+            dma((count, grid - 1)),
+            dma((count, grid - 1)),
+            dma((count, grid - 1)),
+            dma((count, grid - 1)),
+            dma((count, nz - 1)),
+            dma((count, nz - 1)),
+            dma((count, nz - 1)),
+            dma((count, nz - 1)),
         ],
         compiler_params=pltpu.CompilerParams(
             collective_id=0, has_side_effects=True, vmem_limit_bytes=VMEM_BYTES
@@ -398,7 +446,7 @@
         tile_rows[0], tile_cols[0], self_blocks[0], feats, adj, weight, proj_bias[None],
         cotangent[0],
     )
-    return (hidden[None], weight_grad.astype(jnp.float32))
+    return (hidden[None], weight_grad)
 
 
 def solution(mesh):

time: 85.6 us -> 86.5 us (1.011)
  other arithmetic: 1.96 us -> 0 us
  Pallas kernels: 79.7 us -> 81.6 us
  local copies, waits for them, and re-layouts: 3.08 us -> 4.04 us
    convert_element_type x1 -> x0, other arithmetic: 1.96 us -> none  [per_device(): return (hidden[None], weight_grad.astype(jnp.float32))]
    pallas_call x1, Pallas kernels: 79.7 us -> 81.6 us  [per_device(): pl.pallas_call(functools.partial(layer_kernel, n, nz), out_shape=(jax.Sha...]
    unnamed x1 -> x4, local copies, waits for them, and re-layouts: 3.08 us -> 4.04 us
where the time goes in v3:
time: 86.5 us; the launch traced here: 86.3 us
  Pallas kernels  81.6 us (94%)
  local copies, waits for them, and re-layouts  4.04 us (5%)
    pallas_call x1, Pallas kernels, per_device(): pl.pallas_call(functools.partial(layer_kernel, n, nz), out_shape=(jax.Sha...  81.6 us
    unnamed x4, local copies, waits for them, and re-layouts  4.04 us

profile of v3, /device:TPU:0, one launch (start us, length us, event | category | flops | bytes accessed | tf_op | source)
XLA Modules:
  0.0 86.3 jit_solution(5628448495708619693)
XLA Ops:
  0.6 81.6 %layer.1 = (bf16[1024,1024]{1,0:T(8,128)(2,1)}, f32[192,1024]{1,0:T(8,128)}) custom-call(s32[96]{0:T(128)} %bitcast.13, s32[96]{0:T(128)} %bitcast.14, s32[64]{0:T(128)} %bitcast.15, bf16[192,96,128]{2,1,0:T(8,128)(2,1)} %bitcast.8, bf16[96,128,128]{2,1,0:T(8,128)(2,1)} %bitcast.9, bf16[1536,1024]{1,0:T(8,128)(2,1)} %w_hbm.1, f32[1,1024]{1,0:T(1,128)} %bitcast.12, ...), custom_call_target="tpu_custom_call" | custom-call | tf_op jit(solution)/shard_map/layer/pallas_call | solution.py:392
  82.3 0.0 copy-start
  82.3 3.2 %copy.12 = bf16[1,1024,1024]{2,1,0:T(8,128)(2,1)} copy(bf16[1,1024,1024]{2,1,0:T(8,128)(2,1)} %bitcast.11) | data formatting | bytes 4194304
  85.4 0.0 copy-done
  85.4 0.9 %copy.13 = f32[192,1024]{1,0:T(8,128)} copy(f32[192,1024]{1,0:T(8,128)S(1)} %copy-done) | data formatting | bytes 1572864
Async XLA Ops:
  82.3 3.2 %copy-start = (f32[192,1024]{1,0:T(8,128)S(1)}, f32[192,1024]{1,0:T(8,128)}, u32[]{:S(2)}) copy-start(f32[192,1024]{1,0:T(8,128)} %get-tuple-element.9) | copy-start | bytes 2359300

commit v4 on v2

--- a/solution.py
+++ b/solution.py
@@ -17,7 +17,7 @@
     n, nz, rows_ref, cols_ref, blocks_ref, feat_hbm, adj_hbm, w_hbm, bias_ref, cot_hbm,
     hid_hbm, grad_ref,
     feat, adj, w, cot, hidden, sendbuf, recvbuf, scan, last, comb_ref,
-    pg, lhs, picked, mine, pair_out, pair_in, own, chip_out, chip_in, red,
+    pg, pre, lhs, picked, mine, pair_out, pair_in, own, chip_out, chip_in, red,
     z_out, z_in, g_out, g_in,
     load_sem, hid_sem, send_sem, recv_sem,
     pair_sem, chip_ssem, chip_rsem, z_ssem, z_rsem, g_ssem, g_rsem,
@@ -49,8 +49,7 @@
             [(feat_hbm, feat), (adj_hbm, adj), (w_hbm, w), (cot_hbm, cot)]
         )
     ]
-    for load in loads:
-        load.start()
+    loads[0].start()
 
     barrier = pltpu.get_barrier_semaphore()
 
@@ -95,37 +94,6 @@
         fill_self(i, carry)
         self_copy(i, me).start()
         return carry
-
-    loads[0].wait()
-    fill_self(1, 0)
-    pl.semaphore_wait(barrier, (n - 1) + (nz - 1))
-    self_copy(1, me).start()
-    lax.fori_loop(2, n, send_self, 0)
-    for r in range(rows):
-        recvbuf[me, 0, r] = feat[blocks_ref[me * rows + r]]
-
-    loads[1].wait()
-
-    def tile_terms(step, carry):
-        for k in range(8):
-            t = step * 8 + k
-            scan[t] = lax.dot_general(
-                feat[cols_ref[t]], adj[t], (((1,), (1,)), ((), ())),
-                preferred_element_type=jnp.float32,
-            )
-        return carry
-
-    lax.fori_loop(0, tiles // 8, tile_terms, 0)
-
-    def running_sums(step, acc):
-        for k in range(8):
-            t = step * 8 + k
-            same = rows_ref[t] == rows_ref[jnp.maximum(t - 1, 0)]
-            acc = scan[t] + jnp.where(same, 1.0, 0.0) * acc
-            scan[t] = acc
-        return acc
-
-    lax.fori_loop(0, tiles // 8, running_sums, jnp.zeros((width, 128), jnp.float32))
 
     def find_last(r, carry):
         at = jnp.int32(0)
@@ -139,6 +107,38 @@
         return carry
 
     lax.fori_loop(0, n * rows, find_last, 0)
+    loads[0].wait()
+    for load in loads[1:]:
+        load.start()
+    fill_self(1, 0)
+    pl.semaphore_wait(barrier, (n - 1) + (nz - 1))
+    self_copy(1, me).start()
+    lax.fori_loop(2, n, send_self, 0)
+    for r in range(rows):
+        recvbuf[me, 0, r] = feat[blocks_ref[me * rows + r]]
+
+    loads[1].wait()
+
+    def tile_terms(step, carry):
+        for k in range(8):
+            t = step * 8 + k
+            scan[t] = lax.dot_general(
+                feat[cols_ref[t]], adj[t], (((1,), (1,)), ((), ())),
+                preferred_element_type=jnp.float32,
+            )
+        return carry
+
+    lax.fori_loop(0, tiles // 8, tile_terms, 0)
+
+    def running_sums(step, acc):
+        for k in range(8):
+            t = step * 8 + k
+            same = rows_ref[t] == rows_ref[jnp.maximum(t - 1, 0)]
+            acc = scan[t] + jnp.where(same, 1.0, 0.0) * acc
+            scan[t] = acc
+        return acc
+
+    lax.fori_loop(0, tiles // 8, running_sums, jnp.zeros((width, 128), jnp.float32))
 
     def send_group(q, carry):
         def send_agg(i, inner):
@@ -168,35 +168,54 @@
         at = pl.ds(pl.multiple_of(q * step_nodes, step_nodes), step_nodes)
         return pltpu.make_async_copy(hidden.at[at], hid_hbm.at[at], hid_sem.at[q])
 
+    half = n * width
+
+    def place(q, kind):
+        base = kind * half
+        for k in range(GROUP):
+            r = q * GROUP + k
+            lanes = pl.ds(pl.multiple_of(r * 128, 128), 128)
+            if width % 16 == 0:
+                for src in range(n):
+                    comb_ref[pl.ds(base + src * width, width), lanes] = recvbuf[src, kind, r]
+            else:
+                whole = jnp.concatenate(
+                    [recvbuf[src, kind, r].astype(jnp.float32) for src in range(n)], axis=0
+                )
+                comb_ref[pl.ds(base, half), lanes] = whole.astype(jnp.bfloat16)
+        at = pl.ds(pl.multiple_of(q * step_nodes, step_nodes), step_nodes)
+        lhs[...] = comb_ref[pl.ds(base, half), at].T
+        return at
+
+    def forward_self(q, carry):
+        at = place(q, 0)
+
+        def self_columns(k, inner):
+            some = pl.ds(pl.multiple_of(k * step_cols, step_cols), step_cols)
+            pre[at, some] = bias_ref[:, some] + jnp.dot(
+                lhs[...], w[:half, some], preferred_element_type=jnp.float32
+            )
+            return inner
+
+        return lax.fori_loop(0, hid // step_cols, self_columns, carry)
+
+    lax.fori_loop(0, groups, forward_self, 0)
+
     def forward(q, carry):
         def wait_agg(i, inner):
             agg_copy(i, q, lax.rem(me - i + n, n)).wait_recv()
             return inner
 
         lax.fori_loop(1, n, wait_agg, 0)
-        for kind in range(2):
-            base = kind * n * width
-            for k in range(GROUP):
-                r = q * GROUP + k
-                lanes = pl.ds(pl.multiple_of(r * 128, 128), 128)
-                if width % 16 == 0:
-                    for src in range(n):
-                        comb_ref[pl.ds(base + src * width, width), lanes] = recvbuf[src, kind, r]
-                else:
-                    whole = jnp.concatenate(
-                        [recvbuf[src, kind, r].astype(jnp.float32) for src in range(n)], axis=0
-                    )
-                    comb_ref[pl.ds(base, n * width), lanes] = whole.astype(jnp.bfloat16)
-
-        at = pl.ds(pl.multiple_of(q * step_nodes, step_nodes), step_nodes)
-        lhs[...] = comb_ref[:, at].T
+        at = place(q, 1)
 
         def forward_columns(k, inner):
             some = pl.ds(pl.multiple_of(k * step_cols, step_cols), step_cols)
-            pre = jnp.dot(lhs[...], w[:, some], preferred_element_type=jnp.float32)
-            pre = pre + bias_ref[:, some]
-            decay = jnp.exp(jnp.minimum(pre, 0.0))
-            hidden[at, some] = jnp.where(pre > 0, pre, decay - 1.0).astype(jnp.bfloat16)
+            value = pre[at, some] + jnp.dot(
+                lhs[...], w[half:, some], preferred_element_type=jnp.float32
+            )
+            decay = jnp.exp(jnp.minimum(value, 0.0))
+            hidden[at, some] = jnp.where(value > 0, value, decay - 1.0).astype(jnp.bfloat16)
             pg[at, some] = (cot[at, some].astype(jnp.float32) * decay).astype(jnp.bfloat16)
             return inner
 
@@ -216,7 +235,7 @@
             some = pl.ds(pl.multiple_of(k * step_cols, step_cols), step_cols)
             out[:, some] = jnp.dot(
                 picked[...], pg[:, some], preferred_element_type=jnp.float32
-            )
+            ).astype(out.dtype)
             return carry
 
         lax.fori_loop(0, hid // step_cols, some_columns, 0)
@@ -259,10 +278,10 @@
     def chip_stage(p):
         terms(p, core, mine)
         pair_copy(p).wait_recv()
-        own[p] = mine[:piece] + pair_in[p, :piece]
+        own[p] = mine[:piece] + pair_in[p, :piece].astype(jnp.float32)
         for i in range(1, nc):
             part = pl.ds(i * piece, piece)
-            chip_out[p, i - 1] = (mine[part] + pair_in[p, part]).astype(jnp.bfloat16)
+            chip_out[p, i - 1] = (mine[part] + pair_in[p, part].astype(jnp.float32)).astype(jnp.bfloat16)
             chip_copy(p, i).start()
 
     def z_stage(p):
@@ -283,12 +302,14 @@
         g_out[p] = total.astype(jnp.bfloat16)
         for i in range(1, nz):
             g_copy(p, i).start()
-        grad_ref[pl.ds(p * piece, piece), columns(mz)] = g_out[p]
+        grad_ref[pl.ds(p * piece, piece), columns(mz)] = g_out[p].astype(jnp.float32)
 
     def last_stage(p):
         for i in range(1, nz):
             g_copy(p, i).wait_recv()
-            grad_ref[pl.ds(p * piece, piece), columns(lax.rem(mz - i + nz, nz))] = g_in[p, i - 1]
+            grad_ref[pl.ds(p * piece, piece), columns(lax.rem(mz - i + nz, nz))] = (
+                g_in[p, i - 1].astype(jnp.float32)
+            )
 
     pair_stage(0)
     pair_stage(1)
@@ -349,7 +370,7 @@
         functools.partial(layer_kernel, n, nz),
         out_shape=(
             jax.ShapeDtypeStruct((nodes, hid), jnp.bfloat16),
-            jax.ShapeDtypeStruct((share, hid), jnp.bfloat16),
+            jax.ShapeDtypeStruct((share, hid), jnp.float32),
         ),
         in_specs=[smem] * 3 + [anywhere] * 3 + [vmem, anywhere],
         out_specs=(anywhere, vmem),
@@ -365,11 +386,12 @@
             pltpu.SMEM((block_count,), jnp.int32),
             pltpu.VMEM((depth, nodes), jnp.bfloat16),
             pltpu.VMEM((nodes, hid), jnp.bfloat16),
-            pltpu.VMEM((step_nodes, depth), jnp.bfloat16),
+            pltpu.VMEM((nodes, hid), jnp.float32),
+            pltpu.VMEM((step_nodes, depth // 2), jnp.bfloat16),
             pltpu.VMEM((nc * piece, nodes), jnp.bfloat16),
             pltpu.VMEM((nc * piece, hid), jnp.float32),
-            pltpu.VMEM((PIECES, nc * piece, hid), jnp.float32),
-            pltpu.VMEM((PIECES, nc * piece, hid), jnp.float32),
+            pltpu.VMEM((PIECES, nc * piece, hid), jnp.bfloat16),
+            pltpu.VMEM((PIECES, nc * piece, hid), jnp.bfloat16),
             pltpu.VMEM((PIECES, piece, hid), jnp.float32),
             pltpu.VMEM((PIECES, nc - 1, piece, hid), jnp.bfloat16),
             pltpu.VMEM((PIECES, nc - 1, piece, hid), jnp.bfloat16),
@@ -398,7 +420,7 @@
         tile_rows[0], tile_cols[0], self_blocks[0], feats, adj, weight, proj_bias[None],
         cotangent[0],
     )
-    return (hidden[None], weight_grad.astype(jnp.float32))
+    return (hidden[None], weight_grad)
 
 
 def solution(mesh):

time: 85.6 us -> 84.9 us (level)
  other arithmetic: 1.96 us -> 0 us
  local copies, waits for them, and re-layouts: 3.08 us -> 4.04 us
    convert_element_type x1 -> x0, other arithmetic: 1.96 us -> none  [per_device(): return (hidden[None], weight_grad.astype(jnp.float32))]
    unnamed x1 -> x4, local copies, waits for them, and re-layouts: 3.08 us -> 4.04 us
where the time goes in v4:
time: 84.9 us; the launch traced here: 84.7 us
  Pallas kernels  80.1 us (94%)
  local copies, waits for them, and re-layouts  4.04 us (5%)
    pallas_call x1, Pallas kernels, per_device(): pl.pallas_call(functools.partial(layer_kernel, n, nz), out_shape=(jax.Sha...  80.1 us
    unnamed x4, local copies, waits for them, and re-layouts  4.04 us

profile of v4, /device:TPU:0, one launch (start us, length us, event | category | flops | bytes accessed | tf_op | source)
XLA Modules:
  0.0 84.7 jit_solution(15917561190177833945)
XLA Ops:
  0.6 80.1 %layer.1 = (bf16[1024,1024]{1,0:T(8,128)(2,1)}, f32[192,1024]{1,0:T(8,128)}) custom-call(s32[96]{0:T(128)} %bitcast.13, s32[96]{0:T(128)} %bitcast.14, s32[64]{0:T(128)} %bitcast.15, bf16[192,96,128]{2,1,0:T(8,128)(2,1)} %bitcast.8, bf16[96,128,128]{2,1,0:T(8,128)(2,1)} %bitcast.9, bf16[1536,1024]{1,0:T(8,128)(2,1)} %w_hbm.1, f32[1,1024]{1,0:T(1,128)} %bitcast.12, ...), custom_call_target="tpu_custom_call" | custom-call | tf_op jit(solution)/shard_map/layer/pallas_call | solution.py:369
  80.7 0.0 copy-start
  80.7 3.2 %copy.12 = bf16[1,1024,1024]{2,1,0:T(8,128)(2,1)} copy(bf16[1,1024,1024]{2,1,0:T(8,128)(2,1)} %bitcast.11) | data formatting | bytes 4194304
  83.9 0.0 copy-done
  83.9 0.9 %copy.13 = f32[192,1024]{1,0:T(8,128)} copy(f32[192,1024]{1,0:T(8,128)S(1)} %copy-done) | data formatting | bytes 1572864
Async XLA Ops:
  80.7 3.2 %copy-start = (f32[192,1024]{1,0:T(8,128)S(1)}, f32[192,1024]{1,0:T(8,128)}, u32[]{:S(2)}) copy-start(f32[192,1024]{1,0:T(8,128)} %get-tuple-element.9) | copy-start | bytes 2359300

commit v5 on v4

--- a/solution.py
+++ b/solution.py
@@ -17,7 +17,7 @@
     n, nz, rows_ref, cols_ref, blocks_ref, feat_hbm, adj_hbm, w_hbm, bias_ref, cot_hbm,
     hid_hbm, grad_ref,
     feat, adj, w, cot, hidden, sendbuf, recvbuf, scan, last, comb_ref,
-    pg, pre, lhs, picked, mine, pair_out, pair_in, own, chip_out, chip_in, red,
+    pg, pre, lhs, picked, acc, mine, pair_out, pair_in, own, chip_out, chip_in, red,
     z_out, z_in, g_out, g_in,
     load_sem, hid_sem, send_sem, recv_sem,
     pair_sem, chip_ssem, chip_rsem, z_ssem, z_rsem, g_ssem, g_rsem,
@@ -223,22 +223,57 @@
         hid_copy(q).start()
         return carry
 
-    lax.fori_loop(0, groups, forward, 0)
-
-    def terms(p, parity, out):
+    def pick(p, parity, at):
         for i in range(nc):
             owner = lax.rem(chip + i, nc) * 2 + parity
-            at = pl.multiple_of(owner * share + p * piece, piece)
-            picked[i * piece:(i + 1) * piece] = comb_ref[pl.ds(at, piece), :]
-
-        def some_columns(k, carry):
-            some = pl.ds(pl.multiple_of(k * step_cols, step_cols), step_cols)
-            out[:, some] = jnp.dot(
-                picked[...], pg[:, some], preferred_element_type=jnp.float32
-            ).astype(out.dtype)
+            place_at = pl.multiple_of(owner * share + p * piece, piece)
+            picked[i * piece:(i + 1) * piece] = comb_ref[pl.ds(place_at, piece), at]
+
+    def group_nodes(q):
+        return pl.ds(pl.multiple_of(q * step_nodes, step_nodes), step_nodes)
+
+    def gather_terms(q, first):
+        at = group_nodes(q)
+
+        def one_part(k, carry):
+            p, whose = k // 2, lax.rem(k, 2)
+            pick(p, jnp.where(whose == 1, core, 1 - core), at)
+
+            def some_columns(h, inner):
+                some = pl.ds(pl.multiple_of(h * step_cols, step_cols), step_cols)
+                term = jnp.dot(picked[...], pg[at, some], preferred_element_type=jnp.float32)
+                if first:
+                    acc[k, :, some] = term
+                else:
+                    acc[k, :, some] += term
+                return inner
+
+            return lax.fori_loop(0, hid // step_cols, some_columns, carry)
+
+        lax.fori_loop(0, 2 * PIECES, one_part, 0)
+
+    def terms(p, whose, out):
+        at = group_nodes(groups - 1)
+        pick(p, core if whose else 1 - core, at)
+
+        def some_columns(h, carry):
+            some = pl.ds(pl.multiple_of(h * step_cols, step_cols), step_cols)
+            term = jnp.dot(picked[...], pg[at, some], preferred_element_type=jnp.float32)
+            out[:, some] = (acc[2 * p + whose, :, some] + term).astype(out.dtype)
             return carry
 
         lax.fori_loop(0, hid // step_cols, some_columns, 0)
+
+    forward(0, 0)
+    gather_terms(0, True)
+
+    def forward_and_terms(q, carry):
+        forward(q, carry)
+        gather_terms(q, False)
+        return carry
+
+    lax.fori_loop(1, groups - 1, forward_and_terms, 0)
+    forward(groups - 1, 0)
 
     def pair_copy(p):
         return pltpu.make_async_remote_copy(
@@ -272,11 +307,11 @@
         return pl.ds(pl.multiple_of(z * cw, cw), cw)
 
     def pair_stage(p):
-        terms(p, 1 - core, pair_out.at[p])
+        terms(p, 0, pair_out.at[p])
         pair_copy(p).start()
 
     def chip_stage(p):
-        terms(p, core, mine)
+        terms(p, 1, mine)
         pair_copy(p).wait_recv()
         own[p] = mine[:piece] + pair_in[p, :piece].astype(jnp.float32)
         for i in range(1, nc):
@@ -388,7 +423,8 @@
             pltpu.VMEM((nodes, hid), jnp.bfloat16),
             pltpu.VMEM((nodes, hid), jnp.float32),
             pltpu.VMEM((step_nodes, depth // 2), jnp.bfloat16),
-            pltpu.VMEM((nc * piece, nodes), jnp.bfloat16),
+            pltpu.VMEM((nc * piece, step_nodes), jnp.bfloat16),
+            pltpu.VMEM((2 * PIECES, nc * piece, hid), jnp.float32),
             pltpu.VMEM((nc * piece, hid), jnp.float32),
             pltpu.VMEM((PIECES, nc * piece, hid), jnp.bfloat16),
             pltpu.VMEM((PIECES, nc * piece, hid), jnp.bfloat16),

time: 84.9 us -> 92.9 us (1.094)
  Pallas kernels: 80.1 us -> 88 us
    pallas_call x1, Pallas kernels: 80.1 us -> 88 us  [per_device(): pl.pallas_call(functools.partial(layer_kernel, n, nz), out_shape=(jax.Sha...]
where the time goes in v5:
time: 92.9 us; the launch traced here: 92.7 us
  Pallas kernels  88 us (95%)
  local copies, waits for them, and re-layouts  4.04 us (4%)
    pallas_call x1, Pallas kernels, per_device(): pl.pallas_call(functools.partial(layer_kernel, n, nz), out_shape=(jax.Sha...  88 us
    unnamed x4, local copies, waits for them, and re-layouts  4.04 us

profile of v5, /device:TPU:0, one launch (start us, length us, event | category | flops | bytes accessed | tf_op | source)
XLA Modules:
  0.0 92.7 jit_solution(1684342071252920496)
XLA Ops:
  0.6 88.0 %layer.1 = (bf16[1024,1024]{1,0:T(8,128)(2,1)}, f32[192,1024]{1,0:T(8,128)}) custom-call(s32[96]{0:T(128)} %bitcast.13, s32[96]{0:T(128)} %bitcast.14, s32[64]{0:T(128)} %bitcast.15, bf16[192,96,128]{2,1,0:T(8,128)(2,1)} %bitcast.8, bf16[96,128,128]{2,1,0:T(8,128)(2,1)} %bitcast.9, bf16[1536,1024]{1,0:T(8,128)(2,1)} %w_hbm.1, f32[1,1024]{1,0:T(1,128)} %bitcast.12, ...), custom_call_target="tpu_custom_call" | custom-call | tf_op jit(solution)/shard_map/layer/pallas_call | solution.py:404
  88.6 0.0 copy-start
  88.6 3.2 %copy.12 = bf16[1,1024,1024]{2,1,0:T(8,128)(2,1)} copy(bf16[1,1024,1024]{2,1,0:T(8,128)(2,1)} %bitcast.11) | data formatting | bytes 4194304
  91.8 0.0 copy-done
  91.8 0.9 copy.13
Async XLA Ops:
  88.6 3.2 %copy-start = (f32[192,1024]{1,0:T(8,128)S(1)}, f32[192,1024]{1,0:T(8,128)}, u32[]{:S(2)}) copy-start(f32[192,1024]{1,0:T(8,128)} %get-tuple-element.9) | copy-start | bytes 2359300

commit v6 on v4

--- a/solution.py
+++ b/solution.py
@@ -35,7 +35,7 @@
     tiles = adj.shape[0]
     groups = rows // GROUP
     step_nodes = GROUP * 128
-    step_cols = 256
+    step_cols = hid // 2
 
     def chip_at(i):
         return lax.rem(chip + i, nc) * 2 + core
@@ -120,15 +120,15 @@
     loads[1].wait()
 
     def tile_terms(step, carry):
-        for k in range(8):
-            t = step * 8 + k
+        for k in range(16):
+            t = step * 16 + k
             scan[t] = lax.dot_general(
                 feat[cols_ref[t]], adj[t], (((1,), (1,)), ((), ())),
                 preferred_element_type=jnp.float32,
             )
         return carry
 
-    lax.fori_loop(0, tiles // 8, tile_terms, 0)
+    lax.fori_loop(0, tiles // 16, tile_terms, 0)
 
     def running_sums(step, acc):
         for k in range(8):
@@ -231,14 +231,9 @@
             at = pl.multiple_of(owner * share + p * piece, piece)
             picked[i * piece:(i + 1) * piece] = comb_ref[pl.ds(at, piece), :]
 
-        def some_columns(k, carry):
-            some = pl.ds(pl.multiple_of(k * step_cols, step_cols), step_cols)
-            out[:, some] = jnp.dot(
-                picked[...], pg[:, some], preferred_element_type=jnp.float32
-            ).astype(out.dtype)
-            return carry
-
-        lax.fori_loop(0, hid // step_cols, some_columns, 0)
+        out[...] = jnp.dot(
+            picked[...], pg[...], preferred_element_type=jnp.float32
+        ).astype(out.dtype)
 
     def pair_copy(p):
         return pltpu.make_async_remote_copy(

time: 84.9 us -> 83.1 us (0.979)
  Pallas kernels: 80.1 us -> 78.2 us
    pallas_call x1, Pallas kernels: 80.1 us -> 78.2 us  [per_device(): pl.pallas_call(functools.partial(layer_kernel, n, nz), out_shape=(jax.Sha...]
where the time goes in v6:
time: 83.1 us; the launch traced here: 82.9 us
  Pallas kernels  78.2 us (94%)
  local copies, waits for them, and re-layouts  4.04 us (5%)
    pallas_call x1, Pallas kernels, per_device(): pl.pallas_call(functools.partial(layer_kernel, n, nz), out_shape=(jax.Sha...  78.2 us
    unnamed x4, local copies, waits for them, and re-layouts  4.04 us

profile of v6, /device:TPU:0, one launch (start us, length us, event | category | flops | bytes accessed | tf_op | source)
XLA Modules:
  0.0 82.9 jit_solution(10927076651251750990)
XLA Ops:
  0.6 78.2 %layer.1 = (bf16[1024,1024]{1,0:T(8,128)(2,1)}, f32[192,1024]{1,0:T(8,128)}) custom-call(s32[96]{0:T(128)} %bitcast.13, s32[96]{0:T(128)} %bitcast.14, s32[64]{0:T(128)} %bitcast.15, bf16[192,96,128]{2,1,0:T(8,128)(2,1)} %bitcast.8, bf16[96,128,128]{2,1,0:T(8,128)(2,1)} %bitcast.9, bf16[1536,1024]{1,0:T(8,128)(2,1)} %w_hbm.1, f32[1,1024]{1,0:T(1,128)} %bitcast.12, ...), custom_call_target="tpu_custom_call" | custom-call | tf_op jit(solution)/shard_map/layer/pallas_call | solution.py:364
  78.9 0.0 copy-start
  78.9 3.2 %copy.12 = bf16[1,1024,1024]{2,1,0:T(8,128)(2,1)} copy(bf16[1,1024,1024]{2,1,0:T(8,128)(2,1)} %bitcast.11) | data formatting | bytes 4194304
  82.0 0.0 copy-done
  82.0 0.9 %copy.13 = f32[192,1024]{1,0:T(8,128)} copy(f32[192,1024]{1,0:T(8,128)S(1)} %copy-done) | data formatting | bytes 1572864
Async XLA Ops:
  78.9 3.2 %copy-start = (f32[192,1024]{1,0:T(8,128)S(1)}, f32[192,1024]{1,0:T(8,128)}, u32[]{:S(2)}) copy-start(f32[192,1024]{1,0:T(8,128)} %get-tuple-element.9) | copy-start | bytes 2359300

commit v7 on v6

--- a/solution.py
+++ b/solution.py
@@ -8,9 +8,12 @@
 from jax.sharding import PartitionSpec as P
 
 MESH = pl.DeviceIdType.MESH
-PIECES = 3
 GROUP = 2
 VMEM_BYTES = 60 * 1024 * 1024
+
+
+def pieces_of(share):
+    return 4 if share % 64 == 0 else 3
 
 
 def layer_kernel(
@@ -28,7 +31,8 @@
     chip, core = me // 2, lax.rem(me, 2)
     sibling = chip * 2 + (1 - core)
     share, hid = grad_ref.shape
-    piece = share // PIECES
+    pieces = pieces_of(share)
+    piece = share // pieces
     cw = hid // nz
     rows = sendbuf.shape[2]
     width = feat.shape[1]
@@ -307,20 +311,18 @@
             )
 
     pair_stage(0)
-    pair_stage(1)
-    chip_stage(0)
-    pair_stage(2)
-    chip_stage(1)
-    chip_stage(2)
-    z_stage(0)
-    z_stage(1)
-    g_stage(0)
-    z_stage(2)
-    g_stage(1)
-    g_stage(2)
-    for p in range(PIECES):
+    for p in range(pieces):
+        if p + 1 < pieces:
+            pair_stage(p + 1)
+        chip_stage(p)
+    for p in range(pieces):
+        z_stage(p)
+        if p:
+            g_stage(p - 1)
+    g_stage(pieces - 1)
+    for p in range(pieces):
         last_stage(p)
-    for p in range(PIECES):
+    for p in range(pieces):
         pair_copy(p).wait_send()
         for i in range(1, nc):
             chip_copy(p, i).wait_send()
@@ -351,7 +353,8 @@
     depth, hid = weight.shape
     nodes = rows * side
     share = depth // n
-    piece = share // PIECES
+    pieces = pieces_of(share)
+    piece = share // pieces
     nc = n // 2
     cw = hid // nz
     groups = rows // GROUP
@@ -385,27 +388,27 @@
             pltpu.VMEM((step_nodes, depth // 2), jnp.bfloat16),
             pltpu.VMEM((nc * piece, nodes), jnp.bfloat16),
             pltpu.VMEM((nc * piece, hid), jnp.float32),
-            pltpu.VMEM((PIECES, nc * piece, hid), jnp.bfloat16),
-            pltpu.VMEM((PIECES, nc * piece, hid), jnp.bfloat16),
-            pltpu.VMEM((PIECES, piece, hid), jnp.float32),
-            pltpu.VMEM((PIECES, nc - 1, piece, hid), jnp.bfloat16),
-            pltpu.VMEM((PIECES, nc - 1, piece, hid), jnp.bfloat16),
-            pltpu.VMEM((PIECES, piece, hid), jnp.float32),
-            pltpu.VMEM((PIECES, nz - 1, piece, cw), jnp.bfloat16),
-            pltpu.VMEM((PIECES, nz - 1, piece, cw), jnp.bfloat16),
-            pltpu.VMEM((PIECES, piece, cw), jnp.bfloat16),
-            pltpu.VMEM((PIECES, nz - 1, piece, cw), jnp.bfloat16),
+            pltpu.VMEM((pieces, nc * piece, hid), jnp.bfloat16),
+            pltpu.VMEM((pieces, nc * piece, hid), jnp.bfloat16),
+            pltpu.VMEM((pieces, piece, hid), jnp.float32),
+            pltpu.VMEM((pieces, nc - 1, piece, hid), jnp.bfloat16),
+            pltpu.VMEM((pieces, nc - 1, piece, hid), jnp.bfloat16),
+            pltpu.VMEM((pieces, piece, hid), jnp.float32),
+            pltpu.VMEM((pieces, nz - 1, piece, cw), jnp.bfloat16),
+            pltpu.VMEM((pieces, nz - 1, piece, cw), jnp.bfloat16),
+            pltpu.VMEM((pieces, piece, cw), jnp.bfloat16),
+            pltpu.VMEM((pieces, nz - 1, piece, cw), jnp.bfloat16),
             dma((4,)),
             dma((groups,)),
             dma((n, 1 + groups)),
             dma((n, 1 + groups)),
-            dma((PIECES, 2)),
-            dma((PIECES, nc - 1)),
-            dma((PIECES, nc - 1)),
-            dma((PIECES, nz - 1)),
-            dma((PIECES, nz - 1)),
-            dma((PIECES, nz - 1)),
-            dma((PIECES, nz - 1)),
+            dma((pieces, 2)),
+            dma((pieces, nc - 1)),
+            dma((pieces, nc - 1)),
+            dma((pieces, nz - 1)),
+            dma((pieces, nz - 1)),
+            dma((pieces, nz - 1)),
+            dma((pieces, nz - 1)),
         ],
         compiler_params=pltpu.CompilerParams(
             collective_id=0, has_side_effects=True, vmem_limit_bytes=VMEM_BYTES

time: 83.1 us -> 81.3 us (0.978)
  Pallas kernels: 78.2 us -> 76.5 us
    pallas_call x1, Pallas kernels: 78.2 us -> 76.5 us  [per_device(): pl.pallas_call(functools.partial(layer_kernel, n, nz), out_shape=(jax.Sha...]
where the time goes in v7:
time: 81.3 us; the launch traced here: 81.1 us
  Pallas kernels  76.5 us (94%)
  local copies, waits for them, and re-layouts  4.04 us (5%)
    pallas_call x1, Pallas kernels, per_device(): pl.pallas_call(functools.partial(layer_kernel, n, nz), out_shape=(jax.Sha...  76.5 us
    unnamed x4, local copies, waits for them, and re-layouts  4.04 us

profile of v7, /device:TPU:0, one launch (start us, length us, event | category | flops | bytes accessed | tf_op | source)
XLA Modules:
  0.0 81.1 jit_solution(13284356411596291184)
XLA Ops:
  0.6 76.5 %layer.1 = (bf16[1024,1024]{1,0:T(8,128)(2,1)}, f32[192,1024]{1,0:T(8,128)}) custom-call(s32[96]{0:T(128)} %bitcast.13, s32[96]{0:T(128)} %bitcast.14, s32[64]{0:T(128)} %bitcast.15, bf16[192,96,128]{2,1,0:T(8,128)(2,1)} %bitcast.8, bf16[96,128,128]{2,1,0:T(8,128)(2,1)} %bitcast.9, bf16[1536,1024]{1,0:T(8,128)(2,1)} %w_hbm.1, f32[1,1024]{1,0:T(1,128)} %bitcast.12, ...), custom_call_target="tpu_custom_call" | custom-call | tf_op jit(solution)/shard_map/layer/pallas_call | solution.py:367
  77.1 0.0 copy-start
  77.1 3.2 %copy.12 = bf16[1,1024,1024]{2,1,0:T(8,128)(2,1)} copy(bf16[1,1024,1024]{2,1,0:T(8,128)(2,1)} %bitcast.11) | data formatting | bytes 4194304
  80.3 0.0 copy-done
  80.3 0.9 %copy.13 = f32[192,1024]{1,0:T(8,128)} copy(f32[192,1024]{1,0:T(8,128)S(1)} %copy-done) | data formatting | bytes 1572864
Async XLA Ops:
  77.1 3.2 %copy-start = (f32[192,1024]{1,0:T(8,128)S(1)}, f32[192,1024]{1,0:T(8,128)}, u32[]{:S(2)}) copy-start(f32[192,1024]{1,0:T(8,128)} %get-tuple-element.9) | copy-start | bytes 2359300
